TPU v7x, 256 devices: a whole 4x4x8 slice. The times are simulated.
256 devices in a mesh: dp: 64 (over x, z, core), inner: 4 (over y).
Axes of the slice: x: 4, y: 4, z: 8, core: 2. Of those that a mesh axis runs over, the one named last changes fastest.
Arguments:
- history: bfloat16 [32768, 1024], P('dp', 'inner'), may hold values from -6 to 6
- out_grad: bfloat16 [32768, 1024], P('dp', 'inner'), may hold values from -16 to 16
- lengths: int32 [64, 8], P('dp'), may hold values from 1 to 256, 512 in all within a row
- w_in: bfloat16 [1024, 4096], P('dp', 'inner'), may hold values from -0.1875 to 0.1875
- w_out: bfloat16 [1024, 1024], P('inner', 'dp'), may hold values from -0.1875 to 0.1875
Outputs:
- output: bfloat16 [32768, 1024], P('dp', 'inner')
- grad_input: float32 [32768, 1024], P('dp', 'inner')
- grad_w_in: float32 [1024, 4096], P('dp', 'inner')
- grad_w_out: float32 [1024, 1024], P('inner', 'dp')
Inputs may be any that keep to these rules, and one draw needn't show every extreme that they name: `lengths`: each row sums to 512; the longest history of every row is exactly 256.
All inputs are finite; a program needn't handle non-finite values.
Results may differ from a plain program's by a relative error of at most 0.01.
Values may be sent and summed in bfloat16 or wider, within the bound.
A program may use at most 64 MiB of HBM per device.

v0:
```python
import jax
import jax.numpy as jnp
from jax import lax
from jax.sharding import PartitionSpec as P

H = 8
DH = 128
MAXLEN = 256


EPSILON = 1e-06


def silu_slope(value_in):
    sigma = jax.nn.sigmoid(value_in)
    return sigma * (1.0 + value_in * (1.0 - sigma))


def normalize(values):
    row_mean = jnp.mean(values, -1, keepdims=True)
    square_mean = jnp.mean(values * values, -1, keepdims=True)
    inverse = lax.rsqrt(square_mean - row_mean * row_mean + EPSILON)
    return ((values - row_mean) * inverse, inverse)


def block_mask(length_row, row_count):
    seg_ends = jnp.cumsum(length_row)
    position = jnp.arange(row_count, dtype=jnp.int32)
    segment = jnp.sum((position[:, None] >= seg_ends[None, :]).astype(jnp.int32), 1)
    return (segment[:, None] == segment[None, :]) & (position[:, None] >= position[None, :])


def shards(history, out_grad, lengths, w_in, w_out):
    row_count = history.shape[0]
    share = history.shape[1]
    full_in, full_grad = (
        lax.all_gather(history, "inner", axis=1, tiled=True),
        lax.all_gather(out_grad, "inner", axis=1, tiled=True),
    )
    w_in_full = lax.all_gather(w_in, "dp", axis=0, tiled=True)
    w_out_full = lax.all_gather(w_out, "dp", axis=1, tiled=True)
    local_heads = w_in_full.shape[1] // (4 * DH)
    width_local = local_heads * DH
    width_all = H * DH
    input_f = full_in.astype(jnp.float32)
    normed_in, inverse_in = normalize(input_f)
    normed_bf = normed_in.astype(jnp.bfloat16)
    hidden = jnp.dot(normed_bf, w_in_full, preferred_element_type=jnp.float32)
    activated = jax.nn.silu(hidden).astype(jnp.bfloat16).reshape(row_count, local_heads, 4, DH)
    gates = activated[:, :, 0]
    values_v = activated[:, :, 1]
    queries = activated[:, :, 2]
    key_rows = activated[:, :, 3]
    allowed = block_mask(lengths[0], row_count)
    score_scale = DH ** (-0.5)
    scores = (
        jnp.einsum("qhd,khd->hqk", queries, key_rows, preferred_element_type=jnp.float32)
        * score_scale
    )
    weights_a = jnp.where(allowed, jax.nn.silu(scores) / MAXLEN, 0.0).astype(jnp.bfloat16)
    attended = jnp.einsum(
        "hqk,khd->qhd", weights_a, values_v, preferred_element_type=jnp.float32
    ).reshape(row_count, width_local)
    att_sums = lax.psum(
        (jnp.sum(attended, 1, keepdims=True), jnp.sum(attended * attended, 1, keepdims=True)),
        "inner",
    )
    att_mean = att_sums[0] / width_all
    att_inverse = lax.rsqrt(att_sums[1] / width_all - att_mean * att_mean + EPSILON)
    att_norm = (attended - att_mean) * att_inverse
    gate_flat = gates.reshape(row_count, width_local).astype(jnp.float32)
    gated = (att_norm * gate_flat).astype(jnp.bfloat16)
    out_term = jnp.dot(gated, w_out_full, preferred_element_type=jnp.float32)
    out_share = lax.psum_scatter(out_term, "inner", scatter_dimension=1, tiled=True)
    output = (history.astype(jnp.float32) + out_share).astype(jnp.bfloat16)
    grad_gated = jnp.dot(full_grad, w_out_full.T, preferred_element_type=jnp.float32)
    w_out_term = jnp.dot(gated.T, full_grad, preferred_element_type=jnp.float32)
    grad_gate = grad_gated * att_norm
    grad_norm = grad_gated * gate_flat
    grad_sums = lax.psum(
        (jnp.sum(grad_norm, 1, keepdims=True), jnp.sum(grad_norm * att_norm, 1, keepdims=True)),
        "inner",
    )
    grad_att = (
        grad_norm - grad_sums[0] / width_all - att_norm * (grad_sums[1] / width_all)
    ) * att_inverse
    grad_att = grad_att.astype(jnp.bfloat16).reshape(row_count, local_heads, DH)
    grad_weights = jnp.einsum(
        "qhd,khd->hqk", grad_att, values_v, preferred_element_type=jnp.float32
    )
    grad_values = jnp.einsum(
        "hqk,qhd->khd", weights_a, grad_att, preferred_element_type=jnp.float32
    )
    grad_scores = jnp.where(allowed, grad_weights * silu_slope(scores) / MAXLEN, 0.0).astype(
        jnp.bfloat16
    )
    grad_queries = score_scale * jnp.einsum(
        "hqk,khd->qhd", grad_scores, key_rows, preferred_element_type=jnp.float32
    )
    grad_keys = score_scale * jnp.einsum(
        "hqk,qhd->khd", grad_scores, queries, preferred_element_type=jnp.float32
    )
    stacked = jnp.stack(
        [grad_gate.reshape(row_count, local_heads, DH), grad_values, grad_queries, grad_keys], 2
    )
    grad_hidden = (stacked.reshape(row_count, local_heads * 4 * DH) * silu_slope(hidden)).astype(
        jnp.bfloat16
    )
    w_in_term = jnp.dot(normed_bf.T, grad_hidden, preferred_element_type=jnp.float32)
    grad_w_in, grad_w_out = (
        lax.psum_scatter(w_in_term, "dp", scatter_dimension=0, tiled=True),
        lax.psum_scatter(w_out_term, "dp", scatter_dimension=1, tiled=True),
    )
    input_term = jnp.dot(grad_hidden, w_in_full.T, preferred_element_type=jnp.float32)
    grad_normed = lax.psum(input_term.astype(jnp.bfloat16), "inner").astype(jnp.float32)
    row_avg = jnp.mean(grad_normed, 1, keepdims=True)
    cross_avg = jnp.mean(grad_normed * normed_in, 1, keepdims=True)
    full_result = (
        full_grad.astype(jnp.float32) + (grad_normed - row_avg - normed_in * cross_avg) * inverse_in
    )
    grad_input = lax.dynamic_slice_in_dim(full_result, lax.axis_index("inner") * share, share, 1)
    return (output, grad_input, grad_w_in, grad_w_out)


def solution(mesh):
    in_specs = (
        P("dp", "inner"),
        P("dp", "inner"),
        P("dp", None),
        P("dp", "inner"),
        P("inner", "dp"),
    )
    out_specs = (P("dp", "inner"), P("dp", "inner"), P("dp", "inner"), P("inner", "dp"))
    return jax.shard_map(shards, mesh=mesh, in_specs=in_specs, out_specs=out_specs, check_vma=False)
```

profile of v0, /device:TPU:1, one launch (start us, length us, event | category | flops | bytes accessed | tf_op | source)
XLA Modules:
  0.0 555.0 jit_solution(1200586640309440795)
XLA Ops:
  7.2 0.7 all-gather.4.cloned.1.call-update
  7.9 0.7 all-gather.6.cloned.1.call-update
  8.7 0.7 all-gather.8.cloned.1.call-update
  9.4 0.8 reduce-window.8
  10.3 0.1 convert_reduce_fusion.2
  10.3 0.2 fusion.4
  10.6 54.7 %all_gather.14 = bf16[256,1024]{0,1:T(8,128)(2,1)S(1)} all-gather(bf16[256,16]{0,1:T(8,128)(2,1)} %param.9), channel_id=1, replica_groups=mesh['dp'=64,'inner'=4] {'dp'}, dimensions={1}, use_global_device_ids=true | all-gather | bytes 532480 | tf_op jit(solution)/shard_map/all_gather | solution.py:41
  65.2 1.6 convert_reduce_fusion
  66.9 56.7 %all-gather.6.cloned.1.call-done = bf16[1024,1024]{1,0:T(8,128)(2,1)} async-done(((bf16[16,1024]{1,0:T(8,128)(2,1)}), bf16[1024,1024]{1,0:T(8,128)(2,1)}) %all-gather.6.cloned.1.call-update) | async-done | bytes 2097168 | tf_op jit(solution)/shard_map/all_gather | solution.py:40
  123.6 4.7 multiply_convert_fusion.1
  128.2 0.5 copy.41
  128.8 0.2 copy.59
  129.0 0.1 copy.46
  129.2 2.3 select_convert_fusion.1
  131.4 1.1 copy-done.1
  132.5 0.5 fusion.10
  133.0 0.1 reduce_sum.84
  133.1 8.9 %all-reduce.1 = (f32[512,1]{0,1:T(1,128)S(1)}, f32[512,1]{0,1:T(1,128)S(1)}) all-reduce(f32[512,1]{0,1:T(1,128)S(1)} %bitcast.111, f32[512,1]{0,1:T(1,128)S(1)} %bitcast.106), channel_id=1, replica_groups=mesh['dp'=64,'inner'=4] {'inner'}, use_global_device_ids=true, to_apply=%region_7.8 | all-reduce | flops 1024 | bytes 8192 | tf_op jit(solution)/shard_map/psum | solution.py:64
  142.0 8.5 %all-gather.8.cloned.1.call-done = bf16[512,1024]{1,0:T(8,128)(2,1)} async-done(((bf16[512,256]{1,0:T(8,128)(2,1)}), bf16[512,1024]{1,0:T(8,128)(2,1)}) %all-gather.8.cloned.1.call-update) | async-done | bytes 1048592 | tf_op jit(solution)/shard_map/all_gather | solution.py:38
  150.5 1.7 fusion.18
  152.2 8.0 %all-reduce = (f32[512,1]{0,1:T(1,128)S(1)}, f32[512,1]{0,1:T(1,128)S(1)}) all-reduce(f32[512,1]{0,1:T(1,128)S(1)} %bitcast.108, f32[512,1]{0,1:T(1,128)S(1)} %bitcast.107), channel_id=1, replica_groups=mesh['dp'=64,'inner'=4] {'inner'}, use_global_device_ids=true, to_apply=%region_12.13 | all-reduce | flops 1024 | bytes 8192 | tf_op jit(solution)/shard_map/psum | solution.py:80
  160.3 0.2 fusion.15
  160.5 1.0 copy-done.2
  161.5 0.3 convolution_bitcast_fusion
  161.8 0.5 copy-done.10
  162.2 1.3 select_convert_fusion
  163.5 0.5 fusion.3
  164.0 0.3 fusion.2
  164.3 0.2 pad_maximum_fusion
  164.5 1.9 copy.51
  166.3 2.1 reshape.79
  168.5 2.5 multiply_convert_fusion
  170.9 1.1 copy-done.5
  172.0 2.3 convolution_convert_fusion
  174.3 0.0 reduce-scatter.4.cloned.1.call-start
  174.4 1.8 fusion.21
  176.2 0.0 reduce-scatter.8.cloned.1.call-start
  176.3 1.5 fusion.22
  177.8 0.0 reduce-scatter.6.cloned.1.call-start
  177.9 4.6 fusion.11
  182.5 43.3 %all-reduce.4.cloned.1.call-done = bf16[512,1024]{1,0:T(8,128)(2,1)} async-done(((bf16[512,1024]{1,0:T(8,128)(2,1)}), bf16[512,1024]{1,0:T(8,128)(2,1)}) %all-reduce.4.cloned.1.call-update) | async-done | bytes 1048592 | tf_op jit(solution)/shard_map/psum | solution.py:115
  225.8 1.6 convert_element_type.63
  227.4 1.0 convert_reduce_fusion.1
  228.3 1.1 fusion.7
  229.4 33.5 %reduce-scatter.4.cloned.1.call-done = f32[512,256]{1,0:T(8,128)} async-done(((f32[512,1024]{1,0:T(8,128)}), f32[512,256]{1,0:T(8,128)}) %reduce-scatter.4.cloned.1.call-update) | async-done | bytes 524304 | tf_op jit(solution)/shard_map/reduce_scatter | solution.py:74
  262.9 1.8 add_convert_fusion
  264.7 136.7 %reduce-scatter.8.cloned.1.call-done = f32[256,16]{0,1:T(8,128)} async-done(((f32[256,1024]{0,1:T(8,128)}), f32[256,16]{0,1:T(8,128)}) %reduce-scatter.8.cloned.1.call-update) | async-done | bytes 16400 | tf_op jit(solution)/shard_map/reduce_scatter | solution.py:112
  401.4 146.8 %reduce-scatter.6.cloned.1.call-done = f32[16,1024]{1,0:T(8,128)} async-done(((f32[1024,1024]{1,0:T(8,128)}), f32[16,1024]{1,0:T(8,128)}) %reduce-scatter.6.cloned.1.call-update) | async-done | bytes 65552 | tf_op jit(solution)/shard_map/reduce_scatter | solution.py:111
  (33 shorter events, 0.3 us)
Async XLA Ops:
  7.2 58.1 %all-gather.4.cloned.1.call-start = ((), (), s32[]{:S(2)}) async-start(), calls=%async_computation.3 | async-start | bytes 1310720 | tf_op jit(solution)/shard_map/all_gather | solution.py:37
  7.9 115.7 %all-gather.6.cloned.1.call-start = ((), (), s32[]{:S(2)}) async-start(), calls=%async_computation.4 | async-start | bytes 2129920 | tf_op jit(solution)/shard_map/all_gather | solution.py:40
  8.6 141.8 %all-gather.8.cloned.1.call-start = ((), (), s32[]{:S(2)}) async-start(), calls=%async_computation.6 | async-start | bytes 1310720 | tf_op jit(solution)/shard_map/all_gather | solution.py:38
  9.4 216.4 %all-reduce.4.cloned.1.call-start = ((), (), s32[]{:S(2)}) async-start(), calls=%async_computation.7 | async-start | bytes 2097152 | tf_op jit(solution)/shard_map/psum | solution.py:115
  10.6 118.6 %copy-start.7 = (pred[512,512]{1,0:T(8,128)(4,1)}, pred[512,512]{1,0:T(8,128)(4,1)S(1)}, u32[]{:S(2)}) copy-start(pred[512,512]{1,0:T(8,128)(4,1)S(1)} %fusion.4) | copy-start | bytes 786436
  131.4 1.1 copy-start.1
  160.2 1.2 copy-start.2
  160.2 1.5 copy-start.8
  160.3 2.0 copy-start.10
  168.4 3.6 copy-start.9
  170.9 1.1 copy-start.5
  174.3 88.6 %reduce-scatter.4.cloned.1.call-start = ((), (), s32[]{:S(2)}) async-start(), calls=%async_computation.5 | async-start | bytes 2621440 | tf_op jit(solution)/shard_map/reduce_scatter | solution.py:74
  174.4 1.9 copy-start
  176.2 1.7 copy-start.4
  176.2 225.2 %reduce-scatter.8.cloned.1.call-start = ((), (), s32[]{:S(2)}) async-start(), calls=%async_computation.9 | async-start | bytes 1064960 | tf_op jit(solution)/shard_map/reduce_scatter | solution.py:112
  177.8 370.4 %reduce-scatter.6.cloned.1.call-start = ((), (), s32[]{:S(2)}) async-start(), calls=%async_computation.8 | async-start | bytes 4259840 | tf_op jit(solution)/shard_map/reduce_scatter | solution.py:111
  225.8 1.6 copy-start.3
  227.3 35.6 %copy-start.6 = (bf16[512,256]{1,0:T(8,128)(2,1)S(1)}, bf16[512,256]{1,0:T(8,128)(2,1)}, u32[]{:S(2)}) copy-start(bf16[512,256]{1,0:T(8,128)(2,1)} %param.5) | copy-start | bytes 786436
Sparse Core Ops, SparseCore 0:
  9.8 31.3 all-gather.3
  44.0 79.5 all-gather.5
  125.4 25.0 all-gather.7
  174.4 51.2 all-reduce.3
  228.3 34.5 reduce-scatter.3
  267.4 134.0 reduce-scatter.7
  406.1 142.0 reduce-scatter.5
where the time goes:
time: 560 us; the launch traced here: 555 us
  waiting for transfers between devices  428 us (76%)
  blocking collectives  71.6 us (13%)
  matrix products  21.7 us (4%)
  between operations  14.4 us (3%)
  other arithmetic  11.1 us (2%)
  local copies, waits for them, and re-layouts  8.45 us (2%)
    reduce_scatter x1, waiting for transfers between devices, shards(): lax.psum_scatter(w_in_term, 'dp', scatter_dimension=0, tiled=True)  147 us
    reduce_scatter x1, waiting for transfers between devices, shards(): lax.psum_scatter(w_out_term, 'dp', scatter_dimension=1, tiled=True)  137 us
    all_gather x1, waiting for transfers between devices, shards(): w_in_full = lax.all_gather(w_in, 'dp', axis=0, tiled=True)  56.7 us
    all_gather x1, blocking collectives, shards(): w_out_full = lax.all_gather(w_out, 'dp', axis=1, tiled=True)  54.7 us
    psum x1, waiting for transfers between devices, shards(): lax.psum(input_term.astype(jnp.bfloat16), 'inner').astype(jnp.float32)  43.3 us
    reduce_scatter x1, waiting for transfers between devices, shards(): lax.psum_scatter(out_term, 'inner', scatter_dimension=1, tiled=True)  33.5 us
  transfers between devices with their start and end apart: 7, of which 6 were waited for; matrix products, arithmetic and copies ran while one was open for 4% of the time, Pallas kernels for 0%

commit v1 on v0

v1 whole, which is shorter than its diff:
```python
import functools

import jax
import jax.numpy as jnp
from jax import lax
from jax.experimental import pallas as pl
from jax.experimental.pallas import tpu as pltpu
from jax.sharding import PartitionSpec as P

H = 8
DH = 128
MAXLEN = 256
EPSILON = 1e-06
SCALE = DH ** (-0.5)
F32 = jnp.float32
BF16 = jnp.bfloat16
NX = 4
NY = 4
N_SEM = 320

WO, GATE, QUERY, KEY, VALUE, COLS = 0, 256, 512, 768, 1024, 1280
EARLY_A, EARLY_B = (0, 256), (256, 512)
LATE_A, LATE_B = (512, 896), (896, 1280)


def nn(a, b):
    return lax.dot_general(a, b, (((1,), (0,)), ((), ())), preferred_element_type=F32)


def nt(a, b):
    return lax.dot_general(a, b, (((1,), (1,)), ((), ())), preferred_element_type=F32)


def tn(a, b):
    return lax.dot_general(a, b, (((0,), (0,)), ((), ())), preferred_element_type=F32)


class Links:
    def __init__(self, send_sem, recv_sem):
        self.send_sem, self.recv_sem, self.used, self.sent = send_sem, recv_sem, 0, []

    def send(self, source, target, device):
        index = self.used
        self.used += 1
        copy = pltpu.make_async_remote_copy(
            src_ref=source,
            dst_ref=target,
            send_sem=self.send_sem.at[index],
            recv_sem=self.recv_sem.at[index],
            device_id=device,
            device_id_type=pl.DeviceIdType.MESH,
        )
        copy.start()
        self.sent.append((copy, index))
        return index, device

    def arrived(self, handle, region):
        index, device = handle
        pltpu.make_async_remote_copy(
            src_ref=region,
            dst_ref=region,
            send_sem=self.send_sem.at[index],
            recv_sem=self.recv_sem.at[index],
            device_id=device,
            device_id_type=pl.DeviceIdType.MESH,
        ).wait_recv()

    def drain(self):
        for copy, _ in self.sent:
            copy.wait_send()


class RingGather:
    def __init__(self, links, view, right, left, source=None):
        self.links, self.view, self.right, self.left = links, view, right, left
        self.source = source or (lambda half: view(0, half))

    def start(self):
        send, view, source = self.links.send, self.view, self.source
        self.r0 = send(source(0), view(0, 0), self.right)
        self.l1 = send(source(1), view(0, 1), self.left)
        self.r1 = send(source(1), view(0, 1), self.right)
        self.l0 = send(source(0), view(0, 0), self.left)

    def forward(self):
        links, view = self.links, self.view
        links.arrived(self.r0, view(3, 0))
        self.fr = links.send(view(3, 0), view(3, 0), self.right)
        links.arrived(self.l1, view(1, 1))
        self.fl = links.send(view(1, 1), view(1, 1), self.left)

    def near(self):
        links, view = self.links, self.view
        links.arrived(self.r1, view(3, 1))
        links.arrived(self.l0, view(1, 0))

    def far(self):
        links, view = self.links, self.view
        links.arrived(self.fr, view(2, 0))
        links.arrived(self.fl, view(2, 1))


class RingSum:
    def __init__(self, links, part, out_buf, in_buf, right, left):
        self.links, self.part, self.out, self.inn = links, part, out_buf, in_buf
        self.right, self.left = right, left

    def push(self, slot, value, device):
        self.out[slot] = value.astype(BF16)
        return self.links.send(self.out.at[slot], self.inn.at[slot], device)

    def start_far(self):
        self.h0 = self.push(0, self.part(2, 0), self.right)
        self.h1 = self.push(1, self.part(2, 1), self.left)

    def start_right(self):
        self.h2 = self.push(2, self.part(1, 1), self.right)

    def start_left(self):
        self.h3 = self.push(3, self.part(3, 0), self.left)

    def middle(self):
        self.links.arrived(self.h0, self.inn.at[0])
        self.h4 = self.push(4, self.inn[0].astype(F32) + self.part(1, 0), self.right)
        self.links.arrived(self.h1, self.inn.at[1])
        self.h5 = self.push(5, self.inn[1].astype(F32) + self.part(3, 1), self.left)

    def finish(self):
        for handle, slot in ((self.h2, 2), (self.h3, 3), (self.h4, 4), (self.h5, 5)):
            self.links.arrived(handle, self.inn.at[slot])
        first = self.part(0, 0) + self.inn[4].astype(F32) + self.inn[3].astype(F32)
        second = self.part(0, 1) + self.inn[2].astype(F32) + self.inn[5].astype(F32)
        return first, second


def kernel(
    nz,
    history,
    out_grad,
    lengths,
    w_in,
    w_out,
    output,
    grad_input,
    grad_w_in,
    grad_w_out,
    xg,
    dg,
    xh,
    xt,
    dt,
    wg,
    hid,
    slope,
    act,
    mask,
    weights,
    sslope,
    att,
    gg,
    ga,
    gated,
    gh,
    sgrad,
    term,
    sib_out,
    sib_in,
    oterm,
    iterm,
    row_stat,
    st_own,
    st_in,
    st2_own,
    st2_in,
    yo_out,
    yo_in,
    yi_out,
    yi_in,
    wo_tmp,
    wo_back,
    ax_e,
    az_e,
    bz_e,
    bx_e,
    ax_l,
    az_l,
    bz_l,
    bx_l,
    send_sem,
    recv_sem,
    local_sem,
):
    tok, share = history.shape
    half_tok = tok // 2
    width = share * NY
    me = lax.axis_index("dp")
    y = lax.axis_index("inner")
    core = lax.rem(me, 2)
    z = lax.rem(lax.div(me, 2), nz)
    x = lax.div(me, 2 * nz)
    other = 1 - core

    def at_x(k):
        return lax.rem(x + k, NX)

    def at_z(k):
        return lax.rem(z + k, nz)

    def at_y(k):
        return lax.rem(y + k, NY)

    def dev_x(k):
        return {"dp": (at_x(k) * nz + z) * 2 + core}

    def dev_z(k):
        return {"dp": (x * nz + at_z(k)) * 2 + core}

    def dev_y(k):
        return {"inner": at_y(k)}

    sibling = {"dp": (x * nz + z) * 2 + other}
    links = Links(send_sem, recv_sem)

    barrier = pltpu.get_barrier_semaphore()
    partners = (
        [sibling]
        + [dev_y(k) for k in (1, 2, 3)]
        + [dev_x(k) for k in (1, 2, 3)]
        + [dev_z(k) for k in range(1, nz)]
    )
    for device in partners:
        pl.semaphore_signal(barrier, inc=1, device_id=device, device_id_type=pl.DeviceIdType.MESH)

    own_x = pltpu.make_async_copy(history, xg.at[y], local_sem.at[0])
    own_d = pltpu.make_async_copy(out_grad, dg.at[y], local_sem.at[1])
    own_x.start()
    own_d.start()
    wo_tmp[...] = jnp.zeros(wo_tmp.shape, F32)
    wo_tmp[:, 0:16] = w_out[...].astype(F32)
    mine = (x, z, core)
    wg[mine + (slice(None), slice(WO, WO + 256))] = wo_tmp[...].T[0:16, :].astype(BF16)
    for head in range(2):
        for part, base in enumerate((GATE, VALUE, QUERY, KEY)):
            source = head * 4 * DH + part * DH
            target = base + head * DH
            wg[mine + (slice(None), slice(target, target + DH))] = w_in[:, source : source + DH]
    pl.semaphore_wait(barrier, len(partners))

    def rows_of(half):
        return pl.ds(half * half_tok, half_tok)

    gather_x = RingGather(
        links,
        lambda k, half: xg.at[at_y(k), rows_of(half)],
        dev_y(1),
        dev_y(3),
        lambda half: history.at[rows_of(half)],
    )
    gather_d = RingGather(
        links,
        lambda k, half: dg.at[at_y(k), rows_of(half)],
        dev_y(1),
        dev_y(3),
        lambda half: out_grad.at[rows_of(half)],
    )

    n_right = nz // 2
    n_left = nz - 1 - n_right

    class WeightGather:
        def __init__(self, a, b):
            self.ca, self.cb = pl.ds(a[0], a[1] - a[0]), pl.ds(b[0], b[1] - b[0])
            self.shared = []

        def share(self, view):
            region = view(core)
            self.shared.append((links.send(region, region, sibling), view(other)))

        def start(self):
            own_b = wg.at[x, z, core, :, self.cb]
            own_a = wg.at[x, z, core, :, self.ca]
            self.bx = [links.send(own_b, own_b, dev_x(k)) for k in (1, 3, 2)]
            self.az = [(k, links.send(own_a, own_a, dev_z(k))) for k in range(1, nz)]

        def slab_b(self, zz, cc):
            return wg.at[:, zz, cc, :, self.cb]

        def start_b(self):
            for k, handle in zip((1, 3, 2), self.bx):
                links.arrived(handle, wg.at[at_x(NX - k), z, core, :, self.cb])
            region = self.slab_b(z, core)
            self.right = links.send(region, region, dev_z(1))
            if n_left:
                self.left = links.send(region, region, dev_z(nz - 1))
            self.share(lambda cc: self.slab_b(z, cc))
            self.step = 0

        def step_b(self):
            s = self.step
            self.step += 1
            if s < n_right:
                zz = at_z(nz - 1 - s)
                region = self.slab_b(zz, core)
                links.arrived(self.right, region)
                if s + 1 < n_right:
                    self.right = links.send(region, region, dev_z(1))
                self.share(lambda cc: self.slab_b(zz, cc))
            if s < n_left:
                zl = at_z(1 + s)
                region = self.slab_b(zl, core)
                links.arrived(self.left, region)
                if s + 1 < n_left:
                    self.left = links.send(region, region, dev_z(nz - 1))
                self.share(lambda cc: self.slab_b(zl, cc))

        def view_a(self, k, half, cc):
            return wg.at[at_x(k), pl.ds(half * (nz // 2), nz // 2), cc, :, self.ca]

        def start_a(self):
            for k, handle in self.az:
                links.arrived(handle, wg.at[x, at_z(nz - k), core, :, self.ca])
            self.ring = RingGather(
                links, lambda k, half: self.view_a(k, half, core), dev_x(1), dev_x(3)
            )
            self.ring.start()
            self.share(lambda cc: wg.at[x, :, cc, :, self.ca])

        def forward_a(self):
            self.ring.forward()
            self.share(lambda cc: self.view_a(3, 0, cc))
            self.share(lambda cc: self.view_a(1, 1, cc))

        def near_a(self):
            self.ring.near()
            self.share(lambda cc: self.view_a(3, 1, cc))
            self.share(lambda cc: self.view_a(1, 0, cc))

        def far_a(self):
            self.ring.far()
            self.share(lambda cc: self.view_a(2, 0, cc))
            self.share(lambda cc: self.view_a(2, 1, cc))

        def finish(self):
            for handle, region in self.shared:
                links.arrived(handle, region)

    late = WeightGather(LATE_A, LATE_B)
    early = WeightGather(EARLY_A, EARLY_B)
    gather_x.start()
    late.start()
    early.start()

    blocks = tok // 128
    ends = []
    total = jnp.int32(0)
    for k in range(8):
        total = total + lengths[0, k]
        ends.append(total)
    for i in range(blocks):
        row = lax.broadcasted_iota(jnp.int32, (128, 128), 0) + i * 128
        begin = jnp.zeros((128, 128), jnp.int32)
        for k in range(7):
            begin = jnp.where(row >= ends[k], ends[k], begin)
        for j in range(max(0, i - 2), i + 1):
            col = lax.broadcasted_iota(jnp.int32, (128, 128), 1) + j * 128
            allowed = (col >= begin) & (col <= row)
            mask[i * 128 : (i + 1) * 128, j * 128 : (j + 1) * 128] = jnp.where(
                allowed, 1.0 / MAXLEN, 0.0
            ).astype(F32)

    late.start_b()
    late.start_a()
    gather_x.forward()
    early.start_b()
    early.start_a()
    late.step_b()
    late.forward_a()
    own_x.wait()
    gather_x.near()
    gather_x.far()
    gather_d.start()
    late.step_b()

    def norm_rows(block, carry):
        rows = pl.ds(pl.multiple_of(block * 128, 128), 128)
        cols = [xg[k, rows, :].astype(F32) for k in range(NY)]
        mean = sum(jnp.sum(part, 1, keepdims=True) for part in cols) / width
        square = sum(jnp.sum(part * part, 1, keepdims=True) for part in cols) / width
        inverse = lax.rsqrt(square - mean * mean + EPSILON)
        row_stat[0, rows, :] = jnp.broadcast_to(mean, (128, 128))
        row_stat[1, rows, :] = jnp.broadcast_to(inverse, (128, 128))
        for k in range(NY):
            xh[rows, k * share : (k + 1) * share] = ((cols[k] - mean) * inverse).astype(BF16)
        return carry

    lax.fori_loop(0, blocks, norm_rows, 0)
    late.near_a()
    late.step_b()
    early.step_b()
    early.forward_a()
    for k in range(NX):
        turned = xh[:, k * share : (k + 1) * share].T
        xt[k] = turned.reshape(nz, 2, 16, tok)
    late.far_a()
    late.step_b()
    late.finish()
    early.step_b()
    early.near_a()

    def weight_cols(first, count):
        return wg[:, :, :, :, pl.ds(first, count)].reshape(width, count)

    def hidden_cols(chunk, carry):
        base = pl.multiple_of(chunk * 256, 256)
        block = wg[:, :, :, :, pl.ds(pl.multiple_of(base + GATE, 256), 256)].reshape(width, 256)
        for half in range(2):
            rows = pl.ds(half * half_tok, half_tok)
            value = nn(xh[rows, :], block)
            sigma = jax.nn.sigmoid(value)
            cols = pl.ds(base, 256)
            hid[rows, cols] = value
            act[rows, cols] = (value * sigma).astype(BF16)
            slope[rows, cols] = sigma * (1.0 + value * (1.0 - sigma))
        return carry

    lax.fori_loop(1, 4, hidden_cols, 0)
    gather_d.forward()
    early.step_b()
    early.far_a()
    early.step_b()

    def part_of(ref, base, head, rows):
        first = base - GATE + head * DH
        return ref[rows, first : first + DH]

    def band(i):
        return slice(i * 128, (i + 1) * 128), slice(max(0, i - 2) * 128, (i + 1) * 128)

    for head in range(2):
        for i in range(blocks):
            rows, cols = band(i)
            score = nt(part_of(act, QUERY, head, rows), part_of(act, KEY, head, cols)) * SCALE
            sigma = jax.nn.sigmoid(score)
            seen = mask[rows, cols]
            soft = score * sigma
            weight = (soft * seen).astype(BF16)
            weights[head, rows, cols] = weight
            sslope[head, rows, cols] = sigma * (1.0 + score * (1.0 - sigma)) * seen
            att[rows, head * DH : (head + 1) * DH] = nn(weight, part_of(act, VALUE, head, cols))

    early.finish()
    lax.fori_loop(0, 1, hidden_cols, 0)
    own_d.wait()
    gather_d.near()
    gather_d.far()
    for half in range(2):
        rows = pl.ds(half * half_tok, half_tok)
        total_gg = None
        for k in range(NY):
            block = wg[k, :, :, :, WO : WO + 256].reshape(share, 256)
            piece = nn(dg[k, rows, :], block)
            total_gg = piece if total_gg is None else total_gg + piece
        gg[rows, :] = total_gg

    def columns_sum(value):
        return jnp.sum(value.T, 0, keepdims=True)

    def gate_of(head):
        return part_of(act, GATE, head, slice(None)).astype(F32)

    def head_cols(head):
        return slice(head * DH, (head + 1) * DH)

    sums = [0.0] * 4
    for head in range(2):
        a = att[:, head_cols(head)]
        g = gg[:, head_cols(head)] * gate_of(head)
        for k, term_k in enumerate((a, a * a, g, g * a)):
            sums[k] = sums[k] + term_k
    for k in range(4):
        st_own[k : k + 1, :] = columns_sum(sums[k])
    stat = [(k, links.send(st_own, st_in.at[y], dev_y(k))) for k in (1, 3, 2)]
    for k in range(NY):
        dt[k] = dg[k].T.reshape(nz, 2, 16, tok)
    for k, handle in stat:
        links.arrived(handle, st_in.at[at_y(NY - k)])
    st_in[y] = st_own[...]
    sums = st_in[0] + st_in[1] + st_in[2] + st_in[3]

    def spread(row_values):
        return jnp.broadcast_to(row_values, (128, tok)).T

    att_mean = sums[0:1] / (H * DH)
    att_inv = lax.rsqrt(sums[1:2] / (H * DH) - att_mean * att_mean + EPSILON)
    norm_mean = sums[2:3] / (H * DH)
    cross_mean = (sums[3:4] - att_mean * sums[2:3]) * att_inv / (H * DH)
    att_mean, att_inv, norm_mean, cross_mean = (
        spread(value) for value in (att_mean, att_inv, norm_mean, cross_mean)
    )
    for head in range(2):
        cols = head_cols(head)
        att_norm = (att[:, cols] - att_mean) * att_inv
        gate = gate_of(head)
        gated[:, cols] = (att_norm * gate).astype(BF16)
        g = gg[:, cols]
        gh[:, cols] = (g * att_norm * slope[:, cols]).astype(BF16)
        ga[:, cols] = ((g * gate - norm_mean - att_norm * cross_mean) * att_inv).astype(BF16)

    class WeightSum:
        def __init__(self, a, b, ax, az, bz, bx):
            self.first, self.end = a[0], b[1]
            self.a, self.b = a, b
            self.wa, self.wb = a[1] - a[0], b[1] - b[0]
            self.ca, self.cb = slice(*a), slice(*b)
            self.ax, self.az, self.bz, self.bx = ax, az, bz, bx
            self.pairs = []

        def multiply(self, lhs, rhs, first):
            count = rhs.shape[1]
            cols = slice(first, first + count)
            for parity, own in ((other, False), (core, True)):
                rows = lhs[:, :, parity].reshape(width // 2, tok)
                value = nn(rows, rhs).reshape(NX, nz, 16, count)
                if own:
                    term[:, :, :, cols] = value
                else:
                    sib_out[:, :, :, cols] = value.astype(BF16)
                    view = (slice(None), slice(None), slice(None), cols)
                    handle = links.send(sib_out.at[view], sib_in.at[view], sibling)
                    self.pairs.append((handle, view))

        def join(self):
            for handle, view in self.pairs:
                links.arrived(handle, sib_in.at[view])
                term[view] = term[view] + sib_in[view].astype(F32)

        def part_a(self, k, half):
            return term[at_x(k), half * (nz // 2) : (half + 1) * (nz // 2), :, self.ca]

        def part_b(self, k):
            return term[:, at_z(k), :, self.cb]

        def start(self):
            self.ring = RingSum(
                links, self.part_a, self.ax.at[0], self.ax.at[1], dev_x(1), dev_x(3)
            )
            self.ring.start_far()
            self.step = 0
            self.push_right(self.part_b(n_right))
            if n_left:
                self.push_left(self.part_b(nz - n_left))
            self.ring.start_right()
            self.ring.start_left()

        def push_right(self, value):
            s = self.step
            self.bz[0, s] = value.astype(BF16)
            self.right = links.send(self.bz.at[0, s], self.bz.at[1, s], dev_z(1))

        def push_left(self, value):
            s = n_right + self.step
            self.bz[0, s] = value.astype(BF16)
            self.left = links.send(self.bz.at[0, s], self.bz.at[1, s], dev_z(nz - 1))

        def step_b(self):
            s = self.step
            self.step += 1
            if s + 1 < n_right:
                links.arrived(self.right, self.bz.at[1, s])
                self.push_right(self.bz[1, s].astype(F32) + self.part_b(n_right - s - 1))
            if s + 1 < n_left:
                links.arrived(self.left, self.bz.at[1, n_right + s])
                self.push_left(
                    self.bz[1, n_right + s].astype(F32) + self.part_b(nz - n_left + s + 1)
                )

        def middle_a(self):
            self.ring.middle()

        def turn_b(self):
            links.arrived(self.right, self.bz.at[1, n_right - 1])
            value = self.part_b(0) + self.bz[1, n_right - 1].astype(F32)
            if n_left:
                links.arrived(self.left, self.bz.at[1, n_right + n_left - 1])
                value = value + self.bz[1, n_right + n_left - 1].astype(F32)
            term[:, z, :, self.cb] = value
            self.hx = []
            for k in (2, 1, 3):
                self.bx[0, k] = term[at_x(k), z, :, self.cb].astype(BF16)
                self.hx.append((k, links.send(self.bx.at[0, k], self.bx.at[1, k], dev_x(k))))

        def turn_a(self):
            first, second = self.ring.finish()
            term[x, 0 : nz // 2, :, self.ca] = first
            term[x, nz // 2 : nz, :, self.ca] = second
            self.hz = []
            for d in range(nz // 2, 0, -1):
                for k in {d, nz - d}:
                    self.az[0, k] = term[x, at_z(k), :, self.ca].astype(BF16)
                    self.hz.append((k, links.send(self.az.at[0, k], self.az.at[1, k], dev_z(k))))

        def finish(self):
            value_b = term[x, z, :, self.cb]
            for k, handle in self.hx:
                links.arrived(handle, self.bx.at[1, k])
                value_b = value_b + self.bx[1, k].astype(F32)
            value_a = term[x, z, :, self.ca]
            for k, handle in self.hz:
                links.arrived(handle, self.az.at[1, k])
                value_a = value_a + self.az[1, k].astype(F32)
            return value_a, value_b

    sum_e = WeightSum(EARLY_A, EARLY_B, ax_e, az_e, bz_e, bx_e)
    sum_l = WeightSum(LATE_A, LATE_B, ax_l, az_l, bz_l, bx_l)

    def out_block(k):
        block = wg[at_y(k), :, :, :, WO : WO + 256].reshape(share, 256)
        for half in range(2):
            oterm[k, rows_of(half), :] = nt(gated[rows_of(half), :], block)

    ring_o = RingSum(
        links, lambda k, half: oterm[k, rows_of(half), :], yo_out, yo_in, dev_y(1), dev_y(3)
    )
    out_block(2)
    ring_o.start_far()
    sum_e.multiply(dt, gated[...], WO)
    sum_e.multiply(xt, gh[:, 0:256], GATE)
    out_block(1)
    ring_o.start_right()
    out_block(3)
    ring_o.start_left()
    out_block(0)
    sum_e.join()
    sum_e.start()

    def backward(head):
        for i in range(blocks):
            rows, cols = band(i)
            grad_weight = nt(ga[rows, head_cols(head)], part_of(act, VALUE, head, cols))
            grad_score = (grad_weight * sslope[head, rows, cols]).astype(BF16)
            sgrad[head, rows, cols] = grad_score
            grad_q = SCALE * nn(grad_score, part_of(act, KEY, head, cols))
            first = QUERY - GATE + head * DH
            gh[rows, first : first + DH] = (grad_q * part_of(slope, QUERY, head, rows)).astype(BF16)
        for j in range(blocks):
            cols = slice(j * 128, (j + 1) * 128)
            rows = slice(j * 128, min(j + 3, blocks) * 128)
            grad_k = SCALE * tn(sgrad[head, rows, cols], part_of(act, QUERY, head, rows))
            grad_v = tn(weights[head, rows, cols], ga[rows, head_cols(head)])
            for base, value in ((KEY, grad_k), (VALUE, grad_v)):
                first = base - GATE + head * DH
                gh[cols, first : first + DH] = (value * part_of(slope, base, head, cols)).astype(BF16)

    backward(0)
    sum_e.step_b()
    sum_e.middle_a()
    ring_o.middle()
    backward(1)
    sum_e.step_b()
    sum_l.multiply(xt, gh[:, 256:512], QUERY)
    sum_l.multiply(xt, gh[:, 512:768], KEY)
    sum_l.multiply(xt, gh[:, 768:1024], VALUE)
    sum_e.step_b()

    def in_block(k):
        block = wg[at_y(k), :, :, :, GATE:COLS].reshape(share, COLS - GATE)
        for half in range(2):
            iterm[k, rows_of(half), :] = nt(gh[rows_of(half), :], block)

    ring_i = RingSum(
        links, lambda k, half: iterm[k, rows_of(half), :], yi_out, yi_in, dev_y(1), dev_y(3)
    )
    in_block(2)
    ring_i.start_far()
    sum_l.join()
    sum_l.start()
    in_block(1)
    ring_i.start_right()
    in_block(3)
    ring_i.start_left()
    in_block(0)
    sum_e.turn_b()
    sum_e.turn_a()

    w_sum = jnp.zeros((1, COLS - GATE), F32)
    for k in range(NX):
        block = wg[k, :, :, :, GATE:COLS].reshape(share, COLS - GATE).astype(F32)
        w_sum = w_sum + jnp.sum(block, 0, keepdims=True)
    plain, cross = 0.0, 0.0
    for k in range((COLS - GATE) // 128):
        cols = slice(k * 128, (k + 1) * 128)
        piece = gh[:, cols].astype(F32)
        plain = plain + piece * w_sum[:, cols]
        cross = cross + piece * hid[:, cols]
    st2_own[0:1, :] = columns_sum(plain)
    st2_own[1:2, :] = columns_sum(cross)
    stat2 = [(k, links.send(st2_own, st2_in.at[y], dev_y(k))) for k in (1, 3, 2)]
    ring_i.middle()
    sum_l.step_b()
    sum_l.middle_a()

    for half, value in enumerate(ring_o.finish()):
        rows = rows_of(half)
        output[rows, :] = (xg[y, rows, :].astype(F32) + value).astype(BF16)
    sum_l.step_b()
    for k, handle in stat2:
        links.arrived(handle, st2_in.at[at_y(NY - k)])
    st2_in[y] = st2_own[...]
    sums2 = (st2_in[0] + st2_in[1] + st2_in[2] + st2_in[3]) / width
    row_avg, cross_avg = spread(sums2[0:1]), spread(sums2[1:2])
    sum_l.step_b()
    sum_l.turn_a()
    sum_l.turn_b()
    for half, value in enumerate(ring_i.finish()):
        rows = rows_of(half)
        here = slice(half * half_tok, (half + 1) * half_tok)
        for first in range(0, share, 128):
            cols = slice(first, min(first + 128, share))
            lanes = slice(0, cols.stop - cols.start)
            mean, inverse = row_stat[0, rows, lanes], row_stat[1, rows, lanes]
            normed = (xg[y, rows, cols].astype(F32) - mean) * inverse
            centred = value[:, cols] - row_avg[here, lanes] - normed * cross_avg[here, lanes]
            grad_input[rows, cols] = dg[y, rows, cols].astype(F32) + centred * inverse

    wo_part, gate_part = sum_e.finish()
    wo_back[...] = jnp.zeros(wo_back.shape, F32)
    wo_back[0:16, :] = wo_part
    grad_w_out[...] = wo_back[...].T[:, 0:16]
    low, high = sum_l.finish()
    pieces = {
        GATE: gate_part[:, 0:128],
        GATE + DH: gate_part[:, 128:256],
        QUERY: low[:, 0:128],
        QUERY + DH: low[:, 128:256],
        KEY: low[:, 256:384],
        KEY + DH: high[:, 0:128],
        VALUE: high[:, 128:256],
        VALUE + DH: high[:, 256:384],
    }
    for head in range(2):
        for part, base in enumerate((GATE, VALUE, QUERY, KEY)):
            target = head * 4 * DH + part * DH
            grad_w_in[:, target : target + DH] = pieces[base + head * DH]
    links.drain()


def shards(nz, history, out_grad, lengths, w_in, w_out):
    tok, share = history.shape
    width = share * NY
    half = tok // 2
    cols = COLS - GATE
    vmem = pltpu.VMEM
    weight_bufs = []
    for a, b in ((EARLY_A, EARLY_B), (LATE_A, LATE_B)):
        wa, wb = a[1] - a[0], b[1] - b[0]
        weight_bufs += [
            vmem((2, 6, nz // 2, 16, wa), BF16),
            vmem((2, nz, 16, wa), BF16),
            vmem((2, nz - 1, NX, 16, wb), BF16),
            vmem((2, NX, 16, wb), BF16),
        ]
    whole = pl.BlockSpec(memory_space=pltpu.VMEM)
    return pl.pallas_call(
        functools.partial(kernel, nz),
        out_shape=(
            jax.ShapeDtypeStruct((tok, share), BF16),
            jax.ShapeDtypeStruct((tok, share), F32),
            jax.ShapeDtypeStruct(w_in.shape, F32),
            jax.ShapeDtypeStruct(w_out.shape, F32),
        ),
        in_specs=[
            pl.BlockSpec(memory_space=pl.ANY),
            pl.BlockSpec(memory_space=pl.ANY),
            pl.BlockSpec(memory_space=pltpu.SMEM),
            whole,
            whole,
        ],
        out_specs=[whole] * 4,
        scratch_shapes=[
            vmem((NY, tok, share), BF16),
            vmem((NY, tok, share), BF16),
            vmem((tok, width), BF16),
            vmem((NX, nz, 2, 16, tok), BF16),
            vmem((NX, nz, 2, 16, tok), BF16),
            vmem((NX, nz, 2, 16, COLS), BF16),
            vmem((tok, cols), F32),
            vmem((tok, cols), F32),
            vmem((tok, cols), BF16),
            vmem((tok, tok), F32),
            vmem((2, tok, tok), BF16),
            vmem((2, tok, tok), F32),
            vmem((tok, 2 * DH), F32),
            vmem((tok, 2 * DH), F32),
            vmem((tok, 2 * DH), BF16),
            vmem((tok, 2 * DH), BF16),
            vmem((tok, cols), BF16),
            vmem((2, tok, tok), BF16),
            vmem((NX, nz, 16, COLS), F32),
            vmem((NX, nz, 16, COLS), BF16),
            vmem((NX, nz, 16, COLS), BF16),
            vmem((NY, tok, share), F32),
            vmem((NY, tok, share), F32),
            vmem((2, tok, 128), F32),
            vmem((8, tok), F32),
            vmem((NY, 8, tok), F32),
            vmem((8, tok), F32),
            vmem((NY, 8, tok), F32),
            vmem((6, half, share), BF16),
            vmem((6, half, share), BF16),
            vmem((6, half, share), BF16),
            vmem((6, half, share), BF16),
            vmem((2 * DH, 128), F32),
            vmem((128, 2 * DH), F32),
            *weight_bufs,
            pltpu.SemaphoreType.DMA((N_SEM,)),
            pltpu.SemaphoreType.DMA((N_SEM,)),
            pltpu.SemaphoreType.DMA((2,)),
        ],
        compiler_params=pltpu.CompilerParams(
            collective_id=0, has_side_effects=True, vmem_limit_bytes=60 * 1024 * 1024
        ),
    )(history, out_grad, lengths, w_in, w_out)


def solution(mesh):
    nz = mesh.shape["dp"] // (2 * NX)
    in_specs = (
        P("dp", "inner"),
        P("dp", "inner"),
        P("dp", None),
        P("dp", "inner"),
        P("inner", "dp"),
    )
    out_specs = (P("dp", "inner"), P("dp", "inner"), P("dp", "inner"), P("inner", "dp"))
    return jax.shard_map(
        functools.partial(shards, nz), mesh=mesh, in_specs=in_specs, out_specs=out_specs, check_vma=False
    )
```

time: 560 us -> 87 us (0.16)
  the two profiles are of different devices: /device:TPU:1 before, /device:TPU:8 now
where the time goes in v1:
time: 87 us; the launch traced here: 86.8 us
  Pallas kernels  79.9 us (92%)
  local copies, waits for them, and re-layouts  6.23 us (7%)
    pallas_call x1, Pallas kernels, shards(): pl.pallas_call(functools.partial(kernel, nz), out_shape=(jax.ShapeDtypeSt...  79.9 us
    unnamed x8, local copies, waits for them, and re-layouts  4.59 us

profile of v1, /device:TPU:8, one launch (start us, length us, event | category | flops | bytes accessed | tf_op | source)
XLA Modules:
  0.0 86.8 jit_solution(8898581242586543570)
XLA Ops:
  0.6 1.4 %copy.9.w_out = bf16[256,16]{1,0:T(8,128)(2,1)} copy(bf16[256,16]{0,1:T(8,128)(2,1)} %param.9) | data formatting | bytes 16384 | tf_op args[4]
  2.1 79.9 %shard_map.84 = (bf16[512,256]{1,0:T(8,128)(2,1)}, f32[512,256]{1,0:T(8,128)}, f32[16,1024]{1,0:T(8,128)}, f32[256,16]{1,0:T(8,128)}) custom-call(bf16[512,256]{1,0:T(8,128)(2,1)} %history.1, bf16[512,256]{1,0:T(8,128)(2,1)} %out_grad.1, s32[1,8]{1,0:T(1,128)} %lengths.1, bf16[16,1024]{1,0:T(8,128)(2,1)} %w_in.1, bf16[256,16]{1,0:T(8,128)(2,1)} %copy.9.w_out), custom_call_target="tpu_custom_call" | custom-call | tf_op jit(solution)/shard_map/pallas_call | solution.py:763
  81.9 0.0 copy-start
  82.0 1.6 %copy.10 = f32[256,16]{0,1:T(8,128)} copy(f32[256,16]{1,0:T(8,128)} %get-tuple-element.7) | data formatting | bytes 32768 | tf_op jit(solution)/shard_map/pallas_call | solution.py:763
  83.6 1.7 %copy.14 = bf16[512,256]{1,0:T(8,128)(2,1)} copy(bf16[512,256]{1,0:T(8,128)(2,1)} %get-tuple-element.12) | data formatting | bytes 524288
  85.3 0.0 copy-done
  85.3 0.0 copy-start.1
  85.3 0.8 copy.15
  86.1 0.1 copy-done.1
  86.1 0.6 copy.16
Async XLA Ops:
  81.9 3.3 %copy-start = (f32[512,256]{1,0:T(8,128)S(1)}, f32[512,256]{1,0:T(8,128)}, u32[]{:S(2)}) copy-start(f32[512,256]{1,0:T(8,128)} %get-tuple-element.13) | copy-start | bytes 1572868
  85.3 0.9 copy-start.1

commit v2 on v1

v2 whole, which is shorter than its diff:
```python
import functools

import jax
import jax.numpy as jnp
from jax import lax
from jax.experimental import pallas as pl
from jax.experimental.pallas import tpu as pltpu
from jax.sharding import PartitionSpec as P

H = 8
DH = 128
MAXLEN = 256
EPSILON = 1e-06
SCALE = DH ** (-0.5)
F32 = jnp.float32
BF16 = jnp.bfloat16
NX = 4
NY = 4
N_SEM = 64

HEAD = 3 * DH
QUERY, KEY, VALUE = 0, DH, 2 * DH
GATE, WO, COLS = 768, 1024, 1280
Z_ORDER = (4, 3, 5, 2, 6, 1, 7)


def nn(a, b):
    return lax.dot_general(a, b, (((1,), (0,)), ((), ())), preferred_element_type=F32)


def nt(a, b):
    return lax.dot_general(a, b, (((1,), (1,)), ((), ())), preferred_element_type=F32)


def tn(a, b):
    return lax.dot_general(a, b, (((0,), (0,)), ((), ())), preferred_element_type=F32)


class Links:
    def __init__(self, send_sem, recv_sem):
        self.send_sem, self.recv_sem, self.phases = send_sem, recv_sem, []

    def phase(self, region):
        return Phase(self, region)

    def drain(self):
        for phase in self.phases:
            phase.sent()


class Phase:
    def __init__(self, links, region):
        index = len(links.phases)
        assert index < N_SEM
        links.phases.append(self)
        self.sems = dict(send_sem=links.send_sem.at[index], recv_sem=links.recv_sem.at[index])
        self.region = region

    def copy(self, source, target, device):
        return pltpu.make_async_remote_copy(
            src_ref=source,
            dst_ref=target,
            device_id=device,
            device_id_type=pl.DeviceIdType.MESH,
            **self.sems,
        )

    def send(self, source, target, device):
        self.device = device
        self.copy(source, target, device).start()

    def arrived(self):
        self.copy(self.region, self.region, self.device).wait_recv()

    def sent(self):
        self.copy(self.region, self.region, self.device).wait_send()


class RingGather:
    def __init__(self, links, view, right, left, source, both):
        self.links, self.view, self.right, self.left = links, view, right, left
        self.source, self.both = source, both

    def start(self):
        view, source, links = self.view, self.source, self.links
        self.r0, self.l1 = links.phase(view(0, 0)), links.phase(view(0, 1))
        self.second = links.phase(self.both)
        self.r0.send(source(0), view(0, 0), self.right)
        self.l1.send(source(1), view(0, 1), self.left)
        self.second.send(source(1), view(0, 1), self.right)
        self.second.send(source(0), view(0, 0), self.left)

    def forward(self):
        view = self.view
        self.last = self.links.phase(self.both)
        self.r0.arrived()
        self.last.send(view(3, 0), view(3, 0), self.right)
        self.l1.arrived()
        self.last.send(view(1, 1), view(1, 1), self.left)

    def finish(self):
        self.second.arrived()
        self.last.arrived()


class RingSum:
    def __init__(self, links, part, out_buf, in_buf, right, left):
        self.links, self.part, self.out, self.inn = links, part, out_buf, in_buf
        self.right, self.left = right, left

    def push(self, phase, slot, value, device):
        self.out[slot] = value.astype(BF16)
        phase.send(self.out.at[slot], self.inn.at[slot], device)

    def start_far(self):
        links = self.links
        self.p0, self.p1 = links.phase(self.out.at[0]), links.phase(self.out.at[1])
        self.rest = links.phase(self.out.at[2:6])
        self.push(self.p0, 0, self.part(2, 0), self.right)
        self.push(self.p1, 1, self.part(2, 1), self.left)

    def start_right(self):
        self.push(self.rest, 2, self.part(1, 1), self.right)

    def start_left(self):
        self.push(self.rest, 3, self.part(3, 0), self.left)

    def middle(self):
        self.p0.arrived()
        self.push(self.rest, 4, self.inn[0].astype(F32) + self.part(1, 0), self.right)
        self.p1.arrived()
        self.push(self.rest, 5, self.inn[1].astype(F32) + self.part(3, 1), self.left)

    def finish(self):
        self.rest.arrived()
        first = self.part(0, 0) + self.inn[4].astype(F32) + self.inn[3].astype(F32)
        second = self.part(0, 1) + self.inn[2].astype(F32) + self.inn[5].astype(F32)
        return first, second


def kernel(
    nz,
    history,
    out_grad,
    lengths,
    w_in,
    w_out,
    output,
    grad_input,
    grad_w_in,
    grad_w_out,
    xg,
    dg,
    xh,
    xt,
    dt,
    wg,
    hid,
    slope,
    act,
    mask,
    weights,
    sslope,
    att,
    gg,
    ga,
    gated,
    gh,
    sgrad,
    term,
    sib_out,
    sib_in,
    oterm,
    iterm,
    row_stat,
    st_own,
    st_in,
    st2_own,
    st2_in,
    yo_out,
    yo_in,
    yi_out,
    yi_in,
    wsum,
    bufs_e,
    bufs_0,
    bufs_1,
    send_sem,
    recv_sem,
    local_sem,
):
    tok, share = history.shape
    half_tok = tok // 2
    width = share * NY
    me = lax.axis_index("dp")
    y = lax.axis_index("inner")
    core = lax.rem(me, 2)
    z = lax.rem(lax.div(me, 2), nz)
    x = lax.div(me, 2 * nz)
    other = 1 - core

    def at_x(k):
        return lax.rem(x + k, NX)

    def at_z(k):
        return lax.rem(z + k, nz)

    def at_y(k):
        return lax.rem(y + k, NY)

    def dev_x(k):
        return {"dp": (at_x(k) * nz + z) * 2 + core}

    def dev_z(k):
        return {"dp": (x * nz + at_z(k)) * 2 + core}

    def dev_y(k):
        return {"inner": at_y(k)}

    sibling = {"dp": (x * nz + z) * 2 + other}
    links = Links(send_sem, recv_sem)

    barrier = pltpu.get_barrier_semaphore()
    partners = (
        [sibling]
        + [dev_y(k) for k in (1, 2, 3)]
        + [dev_x(k) for k in (1, 2, 3)]
        + [dev_z(k) for k in range(1, nz)]
    )
    for device in partners:
        pl.semaphore_signal(barrier, inc=1, device_id=device, device_id_type=pl.DeviceIdType.MESH)

    own_x = pltpu.make_async_copy(history, xg.at[y], local_sem.at[0])
    own_d = pltpu.make_async_copy(out_grad, dg.at[y], local_sem.at[1])
    own_x.start()
    own_d.start()
    mine = (x, z, core, slice(None))
    wg[mine + (slice(WO, COLS),)] = w_out[...]
    for head in range(2):
        places = (GATE + head * DH, head * HEAD + VALUE, head * HEAD + QUERY, head * HEAD + KEY)
        for part, target in enumerate(places):
            source = (head * 4 + part) * DH
            wg[mine + (slice(target, target + DH),)] = w_in[:, source : source + DH]
    pl.semaphore_wait(barrier, len(partners))

    def rows_of(half):
        return pl.ds(half * half_tok, half_tok)

    gather_x = RingGather(
        links,
        lambda k, half: xg.at[at_y(k), rows_of(half)],
        dev_y(1),
        dev_y(3),
        lambda half: history.at[rows_of(half)],
        xg.at[0],
    )
    gather_d = RingGather(
        links,
        lambda k, half: dg.at[at_y(k), rows_of(half)],
        dev_y(1),
        dev_y(3),
        lambda half: out_grad.at[rows_of(half)],
        dg.at[0],
    )
    z_order = [k for k in Z_ORDER if k < nz] if nz == 8 else list(range(1, nz))
    x_order = (2, 1, 3)

    class WeightGather:
        def __init__(self, first, middle, end):
            self.ca = pl.ds(first, middle - first)
            self.cb = pl.ds(middle, end - middle) if end > middle else None

        def start(self):
            if self.cb:
                own = wg.at[x, z, core, :, self.cb]
                self.bx = links.phase(wg.at[0 : NX - 1, z, core, :, self.cb])
                for k in x_order:
                    self.bx.send(own, own, dev_x(k))
            own = wg.at[x, z, core, :, self.ca]
            self.az = links.phase(wg.at[x, 0 : nz - 1, core, :, self.ca])
            for k in z_order:
                self.az.send(own, own, dev_z(k))

        def turn_b(self):
            if self.cb:
                self.bx.arrived()
                slab = wg.at[:, z, core, :, self.cb]
                self.bz = links.phase(wg.at[:, 0 : nz - 1, core, :, self.cb])
                for k in z_order:
                    self.bz.send(slab, slab, dev_z(k))

        def turn_a(self):
            self.az.arrived()
            slab = wg.at[x, :, core, :, self.ca]
            self.ax = links.phase(wg.at[0 : NX - 1, :, core, :, self.ca])
            for k in x_order:
                self.ax.send(slab, slab, dev_x(k))

        def share(self):
            self.shared = []
            for last, cols in ((self.bz if self.cb else None, self.cb), (self.ax, self.ca)):
                if cols is not None:
                    last.arrived()
                    region = wg.at[:, :, core, :, cols]
                    phase = links.phase(region)
                    phase.send(region, region, sibling)
                    self.shared.append(phase)

        def finish(self):
            for phase in self.shared:
                phase.arrived()

    group_0 = WeightGather(0, 256, HEAD)
    group_1 = WeightGather(HEAD, HEAD + 256, 2 * HEAD)
    group_g = WeightGather(GATE, COLS, COLS)
    group_0.start()
    gather_x.start()
    group_1.start()
    group_g.start()

    blocks = tok // 128
    ends = []
    total = jnp.int32(0)
    for k in range(8):
        total = total + lengths[0, k]
        ends.append(total)
    for i in range(blocks):
        row = lax.broadcasted_iota(jnp.int32, (128, 128), 0) + i * 128
        begin = jnp.zeros((128, 128), jnp.int32)
        for k in range(7):
            begin = jnp.where(row >= ends[k], ends[k], begin)
        for j in range(max(0, i - 2), i + 1):
            col = lax.broadcasted_iota(jnp.int32, (128, 128), 1) + j * 128
            allowed = (col >= begin) & (col <= row)
            mask[i * 128 : (i + 1) * 128, j * 128 : (j + 1) * 128] = jnp.where(
                allowed, 1.0 / MAXLEN, 0.0
            ).astype(F32)

    group_0.turn_b()
    gather_x.forward()
    group_0.turn_a()
    group_1.turn_b()
    group_1.turn_a()
    group_g.turn_a()
    own_x.wait()
    gather_x.finish()
    gather_d.start()

    def norm_rows(block, carry):
        rows = pl.ds(pl.multiple_of(block * 128, 128), 128)
        cols = [xg[k, rows, :].astype(F32) for k in range(NY)]
        mean = sum(jnp.sum(part, 1, keepdims=True) for part in cols) / width
        square = sum(jnp.sum(part * part, 1, keepdims=True) for part in cols) / width
        inverse = lax.rsqrt(square - mean * mean + EPSILON)
        row_stat[0, rows, :] = jnp.broadcast_to(mean, (128, 128))
        row_stat[1, rows, :] = jnp.broadcast_to(inverse, (128, 128))
        for k in range(NY):
            xh[rows, k * share : (k + 1) * share] = ((cols[k] - mean) * inverse).astype(BF16)
        return carry

    lax.fori_loop(0, blocks, norm_rows, 0)
    group_0.share()

    def weight_cols(first, count):
        return wg[:, :, :, :, first : first + count].reshape(width, count)

    def hidden_cols(first, count):
        block = weight_cols(first, count)
        cols = slice(first, first + count)
        for half in range(2):
            rows = rows_of(half)
            value = nn(xh[rows, :], block)
            sigma = jax.nn.sigmoid(value)
            hid[rows, cols] = value
            act[rows, cols] = (value * sigma).astype(BF16)
            slope[rows, cols] = sigma * (1.0 + value * (1.0 - sigma))

    def cols_of(base, head):
        first = head * HEAD + base
        return slice(first, first + DH)

    def band(i):
        return slice(i * 128, (i + 1) * 128), slice(max(0, i - 2) * 128, (i + 1) * 128)

    def forward(head):
        for i in range(blocks):
            rows, cols = band(i)
            score = nt(act[rows, cols_of(QUERY, head)], act[cols, cols_of(KEY, head)]) * SCALE
            sigma = jax.nn.sigmoid(score)
            seen = mask[rows, cols]
            weight = (score * sigma * seen).astype(BF16)
            weights[head, rows, cols] = weight
            sslope[head, rows, cols] = sigma * (1.0 + score * (1.0 - sigma)) * seen
            att[rows, head * DH : (head + 1) * DH] = nn(weight, act[cols, cols_of(VALUE, head)])

    group_0.finish()
    hidden_cols(0, HEAD)
    gather_d.forward()
    group_1.share()
    forward(0)
    group_1.finish()
    hidden_cols(HEAD, HEAD)
    group_g.share()
    forward(1)
    own_d.wait()
    gather_d.finish()
    group_g.finish()
    hidden_cols(GATE, 2 * DH)
    for half in range(2):
        rows = rows_of(half)
        total_gg = None
        for k in range(NY):
            block = wg[k, :, :, :, WO:COLS].reshape(share, 2 * DH)
            piece = nn(dg[k, rows, :], block)
            total_gg = piece if total_gg is None else total_gg + piece
        gg[rows, :] = total_gg

    def columns_sum(value):
        return jnp.sum(value.T, 0, keepdims=True)

    def gate_of(head):
        return act[:, GATE + head * DH : GATE + (head + 1) * DH].astype(F32)

    def head_cols(head):
        return slice(head * DH, (head + 1) * DH)

    sums = [0.0] * 4
    for head in range(2):
        a = att[:, head_cols(head)]
        g = gg[:, head_cols(head)] * gate_of(head)
        for k, term_k in enumerate((a, a * a, g, g * a)):
            sums[k] = sums[k] + term_k
    for k in range(4):
        st_own[k : k + 1, :] = columns_sum(sums[k])
    stat = links.phase(st_in.at[0 : NY - 1])
    for k in x_order:
        stat.send(st_own, st_in.at[y], dev_y(k))
    for k in range(NY):
        cols = slice(k * share, (k + 1) * share)
        xt[k] = xh[:, cols].T.reshape(nz, 2, 16, tok)
        dt[k] = dg[k].T.reshape(nz, 2, 16, tok)
    w_sum = jnp.zeros((1, WO), F32)
    for k in range(NX):
        block = wg[k, :, :, :, 0:WO].reshape(share, WO).astype(F32)
        w_sum = w_sum + jnp.sum(block, 0, keepdims=True)
    wsum[...] = w_sum
    stat.arrived()
    st_in[y] = st_own[...]
    sums = st_in[0] + st_in[1] + st_in[2] + st_in[3]

    def spread(row_values):
        return jnp.broadcast_to(row_values, (128, tok)).T

    att_mean = sums[0:1] / (H * DH)
    att_inv = lax.rsqrt(sums[1:2] / (H * DH) - att_mean * att_mean + EPSILON)
    norm_mean = sums[2:3] / (H * DH)
    cross_mean = (sums[3:4] - att_mean * sums[2:3]) * att_inv / (H * DH)
    att_mean, att_inv, norm_mean, cross_mean = (
        spread(value) for value in (att_mean, att_inv, norm_mean, cross_mean)
    )
    for head in range(2):
        cols = head_cols(head)
        att_norm = (att[:, cols] - att_mean) * att_inv
        gate = gate_of(head)
        gated[:, cols] = (att_norm * gate).astype(BF16)
        g = gg[:, cols]
        here = slice(GATE + head * DH, GATE + (head + 1) * DH)
        gh[:, here] = (g * att_norm * slope[:, here]).astype(BF16)
        ga[:, cols] = ((g * gate - norm_mean - att_norm * cross_mean) * att_inv).astype(BF16)

    class WeightSum:
        def __init__(self, first, middle, end, bufs):
            self.a, self.b = slice(first, middle), slice(middle, end)
            self.all = slice(first, end)
            self.ax, self.az = bufs[0], bufs[1]
            self.bz, self.bx = bufs[2:4] if end > middle else (None, None)

        def multiply(self, products):
            everything = (slice(None), slice(None), slice(None))
            view = everything + (self.all,)
            for parity, own in ((other, False), (core, True)):
                for lhs, rhs, first in products:
                    count = rhs.shape[1]
                    here = everything + (slice(first, first + count),)
                    rows = lhs[:, :, parity].reshape(width // 2, tok)
                    value = nn(rows, rhs).reshape(NX, nz, 16, count)
                    if own:
                        term[here] = value
                    else:
                        sib_out[here] = value.astype(BF16)
                if not own:
                    self.pair = links.phase(sib_in.at[view])
                    self.pair.send(sib_out.at[view], sib_in.at[view], sibling)

        def joined(self, place):
            return term[place] + sib_in[place].astype(F32)

        def join(self):
            self.pair.arrived()
            if self.bz is not None:
                self.pz = links.phase(self.bz.at[0])
                for k in z_order:
                    self.bz[0, k - 1] = self.joined((slice(None), at_z(k), slice(None), self.b)).astype(BF16)
                    self.pz.send(self.bz.at[0, k - 1], self.bz.at[1, k - 1], dev_z(k))
            self.px = links.phase(self.ax.at[0])
            for k in x_order:
                self.ax[0, k - 1] = self.joined((at_x(k), slice(None), slice(None), self.a)).astype(BF16)
                self.px.send(self.ax.at[0, k - 1], self.ax.at[1, k - 1], dev_x(k))

        def turn_b(self):
            if self.bz is None:
                return
            place = (slice(None), z, slice(None), self.b)
            value = self.joined(place)
            self.pz.arrived()
            for k in range(nz - 1):
                value = value + self.bz[1, k].astype(F32)
            term[place] = value
            self.pxb = links.phase(self.bx.at[0])
            for k in x_order:
                self.bx[0, k - 1] = term[at_x(k), z, :, self.b].astype(BF16)
                self.pxb.send(self.bx.at[0, k - 1], self.bx.at[1, k - 1], dev_x(k))

        def turn_a(self):
            place = (x, slice(None), slice(None), self.a)
            value = self.joined(place)
            self.px.arrived()
            for k in range(NX - 1):
                value = value + self.ax[1, k].astype(F32)
            term[place] = value
            self.pza = links.phase(self.az.at[0])
            for k in z_order:
                self.az[0, k - 1] = term[x, at_z(k), :, self.a].astype(BF16)
                self.pza.send(self.az.at[0, k - 1], self.az.at[1, k - 1], dev_z(k))

        def finish(self):
            value_a = term[x, z, :, self.a]
            self.pza.arrived()
            for k in range(nz - 1):
                value_a = value_a + self.az[1, k].astype(F32)
            if self.bz is None:
                return value_a, None
            value_b = term[x, z, :, self.b]
            self.pxb.arrived()
            for k in range(NX - 1):
                value_b = value_b + self.bx[1, k].astype(F32)
            return value_a, value_b

    sum_e = WeightSum(GATE, COLS, COLS, bufs_e)
    sum_0 = WeightSum(0, 256, HEAD, bufs_0)
    sum_1 = WeightSum(HEAD, HEAD + 256, 2 * HEAD, bufs_1)

    def out_block(k):
        block = wg[at_y(k), :, :, :, WO:COLS].reshape(share, 2 * DH)
        for half in range(2):
            oterm[k, rows_of(half), :] = nt(gated[rows_of(half), :], block)

    def backward(head):
        mine_cols = head_cols(head)
        for i in range(blocks):
            rows, cols = band(i)
            grad_weight = nt(ga[rows, mine_cols], act[cols, cols_of(VALUE, head)])
            grad_score = (grad_weight * sslope[head, rows, cols]).astype(BF16)
            sgrad[head, rows, cols] = grad_score
            grad_q = SCALE * nn(grad_score, act[cols, cols_of(KEY, head)])
            here = cols_of(QUERY, head)
            gh[rows, here] = (grad_q * slope[rows, here]).astype(BF16)
        for j in range(blocks):
            cols = slice(j * 128, (j + 1) * 128)
            rows = slice(j * 128, min(j + 3, blocks) * 128)
            grad_k = SCALE * tn(sgrad[head, rows, cols], act[rows, cols_of(QUERY, head)])
            grad_v = tn(weights[head, rows, cols], ga[rows, mine_cols])
            for base, value in ((KEY, grad_k), (VALUE, grad_v)):
                here = cols_of(base, head)
                gh[cols, here] = (value * slope[cols, here]).astype(BF16)

    def in_block(k):
        block = wg[at_y(k), :, :, :, 0:WO].reshape(share, WO)
        for half in range(2):
            iterm[k, rows_of(half), :] = nt(gh[rows_of(half), :], block)

    ring_o = RingSum(
        links, lambda k, half: oterm[k, rows_of(half), :], yo_out, yo_in, dev_y(1), dev_y(3)
    )
    ring_i = RingSum(
        links, lambda k, half: iterm[k, rows_of(half), :], yi_out, yi_in, dev_y(1), dev_y(3)
    )

    sum_e.multiply([(dt, gated[...], WO), (xt, gh[:, GATE:WO], GATE)])
    out_block(2)
    ring_o.start_far()
    out_block(1)
    ring_o.start_right()
    out_block(3)
    ring_o.start_left()
    out_block(0)
    sum_e.join()
    backward(0)
    sum_0.multiply([(xt, gh[:, 0:HEAD], 0)])
    ring_o.middle()
    sum_0.join()
    backward(1)
    sum_1.multiply([(xt, gh[:, HEAD : 2 * HEAD], HEAD)])
    in_block(2)
    ring_i.start_far()
    sum_1.join()
    in_block(1)
    ring_i.start_right()
    in_block(3)
    ring_i.start_left()
    in_block(0)
    sum_e.turn_a()

    plain, cross = 0.0, 0.0
    for k in range(WO // 128):
        cols = slice(k * 128, (k + 1) * 128)
        piece = gh[:, cols].astype(F32)
        plain = plain + piece * wsum[:, cols]
        cross = cross + piece * hid[:, cols]
    st2_own[0:1, :] = columns_sum(plain)
    st2_own[1:2, :] = columns_sum(cross)
    stat2 = links.phase(st2_in.at[0 : NY - 1])
    for k in x_order:
        stat2.send(st2_own, st2_in.at[y], dev_y(k))
    sum_0.turn_b()
    sum_0.turn_a()
    ring_i.middle()
    for half, value in enumerate(ring_o.finish()):
        rows = rows_of(half)
        output[rows, :] = (xg[y, rows, :].astype(F32) + value).astype(BF16)
    sum_1.turn_b()
    sum_1.turn_a()
    stat2.arrived()
    st2_in[y] = st2_own[...]
    sums2 = (st2_in[0] + st2_in[1] + st2_in[2] + st2_in[3]) / width
    row_avg, cross_avg = spread(sums2[0:1]), spread(sums2[1:2])
    gate_part, _ = sum_e.finish()
    grad_w_out[...] = gate_part[:, 256:512]
    pieces = {GATE: gate_part[:, 0:128], GATE + DH: gate_part[:, 128:256]}
    for half, value in enumerate(ring_i.finish()):
        rows = rows_of(half)
        here = slice(half * half_tok, (half + 1) * half_tok)
        for first in range(0, share, 128):
            cols = slice(first, min(first + 128, share))
            lanes = slice(0, cols.stop - cols.start)
            mean, inverse = row_stat[0, rows, lanes], row_stat[1, rows, lanes]
            normed = (xg[y, rows, cols].astype(F32) - mean) * inverse
            centred = value[:, cols] - row_avg[here, lanes] - normed * cross_avg[here, lanes]
            grad_input[rows, cols] = dg[y, rows, cols].astype(F32) + centred * inverse
    for head, group in enumerate((sum_0, sum_1)):
        low, high = group.finish()
        pieces[head * HEAD + QUERY] = low[:, 0:128]
        pieces[head * HEAD + KEY] = low[:, 128:256]
        pieces[head * HEAD + VALUE] = high
    for head in range(2):
        places = (GATE + head * DH, head * HEAD + VALUE, head * HEAD + QUERY, head * HEAD + KEY)
        for part, place in enumerate(places):
            target = (head * 4 + part) * DH
            grad_w_in[:, target : target + DH] = pieces[place]
    links.drain()


def place_kernel(*refs):
    sems = refs[-1]
    count = len(refs) // 2
    copies = [
        pltpu.make_async_copy(refs[i], refs[count + i], sems.at[i]) for i in range(count)
    ]
    for copy in copies:
        copy.start()
    for copy in copies:
        copy.wait()


def shards(nz, history, out_grad, lengths, w_in, w_out):
    tok, share = history.shape
    width = share * NY
    half = tok // 2
    cols = WO
    vmem = pltpu.VMEM
    def sum_bufs(wa, wb):
        out = [vmem((2, NX - 1, nz, 16, wa), BF16), vmem((2, nz - 1, 16, wa), BF16)]
        if wb:
            out += [vmem((2, nz - 1, NX, 16, wb), BF16), vmem((2, NX - 1, 16, wb), BF16)]
        return out

    whole = pl.BlockSpec(memory_space=pltpu.VMEM)
    results = pl.pallas_call(
        functools.partial(kernel, nz),
        out_shape=(
            jax.ShapeDtypeStruct((tok, share), BF16),
            jax.ShapeDtypeStruct((tok, share), F32),
            jax.ShapeDtypeStruct(w_in.shape, F32),
            jax.ShapeDtypeStruct(w_out.shape[::-1], F32),
        ),
        in_specs=[
            pl.BlockSpec(memory_space=pl.ANY),
            pl.BlockSpec(memory_space=pl.ANY),
            pl.BlockSpec(memory_space=pltpu.SMEM),
            whole,
            whole,
        ],
        out_specs=[whole] * 4,
        scratch_shapes=[
            vmem((NY, tok, share), BF16),
            vmem((NY, tok, share), BF16),
            vmem((tok, width), BF16),
            vmem((NX, nz, 2, 16, tok), BF16),
            vmem((NX, nz, 2, 16, tok), BF16),
            vmem((NX, nz, 2, 16, COLS), BF16),
            vmem((tok, cols), F32),
            vmem((tok, cols), F32),
            vmem((tok, cols), BF16),
            vmem((tok, tok), F32),
            vmem((2, tok, tok), BF16),
            vmem((2, tok, tok), F32),
            vmem((tok, 2 * DH), F32),
            vmem((tok, 2 * DH), F32),
            vmem((tok, 2 * DH), BF16),
            vmem((tok, 2 * DH), BF16),
            vmem((tok, cols), BF16),
            vmem((2, tok, tok), BF16),
            vmem((NX, nz, 16, COLS), F32),
            vmem((NX, nz, 16, COLS), BF16),
            vmem((NX, nz, 16, COLS), BF16),
            vmem((NY, tok, share), F32),
            vmem((NY, tok, share), F32),
            vmem((2, tok, 128), F32),
            vmem((8, tok), F32),
            vmem((NY, 8, tok), F32),
            vmem((8, tok), F32),
            vmem((NY, 8, tok), F32),
            vmem((6, half, share), BF16),
            vmem((6, half, share), BF16),
            vmem((6, half, share), BF16),
            vmem((6, half, share), BF16),
            vmem((1, WO), F32),
            sum_bufs(512, 0),
            sum_bufs(256, 128),
            sum_bufs(256, 128),
            pltpu.SemaphoreType.DMA((N_SEM,)),
            pltpu.SemaphoreType.DMA((N_SEM,)),
            pltpu.SemaphoreType.DMA((2,)),
        ],
        compiler_params=pltpu.CompilerParams(
            collective_id=0, has_side_effects=True, vmem_limit_bytes=60 * 1024 * 1024
        ),
    )(history, out_grad, lengths, w_in, w_out.T)
    anywhere = pl.BlockSpec(memory_space=pl.ANY)
    output, grad_input, grad_w_in, grad_w_out = pl.pallas_call(
        place_kernel,
        out_shape=[jax.ShapeDtypeStruct(r.shape, r.dtype) for r in results],
        in_specs=[anywhere] * 4,
        out_specs=[anywhere] * 4,
        scratch_shapes=[pltpu.SemaphoreType.DMA((4,))],
    )(*results)
    return output, grad_input, grad_w_in, grad_w_out.T


def solution(mesh):
    nz = mesh.shape["dp"] // (2 * NX)
    in_specs = (
        P("dp", "inner"),
        P("dp", "inner"),
        P("dp", None),
        P("dp", "inner"),
        P("inner", "dp"),
    )
    out_specs = (P("dp", "inner"), P("dp", "inner"), P("dp", "inner"), P("inner", "dp"))
    return jax.shard_map(
        functools.partial(shards, nz), mesh=mesh, in_specs=in_specs, out_specs=out_specs, check_vma=False
    )
```

time: 87 us -> 87.1 us (level)
  the two profiles are of different devices: /device:TPU:8 before, /device:TPU:1 now
where the time goes in v2:
time: 87.1 us; the launch traced here: 87 us
  Pallas kernels  86.4 us (99%)
    pallas_call x1, Pallas kernels, shards(): pl.pallas_call(functools.partial(kernel, nz), out_shape=(jax.ShapeDtypeSt...  58.9 us
    pallas_call x1, Pallas kernels, shards(): pl.pallas_call(place_kernel, out_shape=[jax.ShapeDtypeStruct(r.shape, r.d...  27.4 us

profile of v2, /device:TPU:1, one launch (start us, length us, event | category | flops | bytes accessed | tf_op | source)
XLA Modules:
  0.0 87.0 jit_solution(945630559922854695)
XLA Ops:
  0.6 58.9 %shard_map.84 = (bf16[512,256]{1,0:T(8,128)(2,1)}, f32[512,256]{1,0:T(8,128)}, f32[16,1024]{1,0:T(8,128)}, f32[16,256]{1,0:T(8,128)}) custom-call(bf16[512,256]{1,0:T(8,128)(2,1)} %history.1, bf16[512,256]{1,0:T(8,128)(2,1)} %out_grad.1, s32[1,8]{1,0:T(1,128)} %lengths.1, bf16[16,1024]{1,0:T(8,128)(2,1)} %w_in.1, bf16[16,256]{1,0:T(8,128)(2,1)} %bitcast.2), custom_call_target="tpu_custom_call" | custom-call | tf_op jit(solution)/shard_map/pallas_call | solution.py:688
  59.5 27.4 %shard_map.85 = (bf16[512,256]{1,0:T(8,128)(2,1)}, f32[512,256]{1,0:T(8,128)}, f32[16,1024]{1,0:T(8,128)}, f32[16,256]{1,0:T(8,128)}) custom-call(bf16[512,256]{1,0:T(8,128)(2,1)} %get-tuple-element.12.refs_0_, f32[512,256]{1,0:T(8,128)} %get-tuple-element.13.refs_1_, f32[16,1024]{1,0:T(8,128)} %get-tuple-element.14.refs_2_, f32[16,256]{1,0:T(8,128)} %get-tuple-element.15.refs_3_), custom_call_target="tpu_custom_call" | custom-call | tf_op jit(solution)/shard_map/pallas_call | solution.py:750

commit v3 on v2

--- a/solution.py
+++ b/solution.py
@@ -16,7 +16,7 @@
 BF16 = jnp.bfloat16
 NX = 4
 NY = 4
-N_SEM = 64
+N_SEM = 47
 
 HEAD = 3 * DH
 QUERY, KEY, VALUE = 0, DH, 2 * DH
@@ -145,6 +145,10 @@
     lengths,
     w_in,
     w_out,
+    output_hbm,
+    grad_input_hbm,
+    grad_w_in_hbm,
+    grad_w_out_hbm,
     output,
     grad_input,
     grad_w_in,
@@ -220,6 +224,13 @@
     sibling = {"dp": (x * nz + z) * 2 + other}
     links = Links(send_sem, recv_sem)
 
+    written = []
+
+    def write(index, source, target):
+        copy = pltpu.make_async_copy(source, target, local_sem.at[2 + index])
+        copy.start()
+        written.append(copy)
+
     barrier = pltpu.get_barrier_semaphore()
     partners = (
         [sibling]
@@ -312,7 +323,7 @@
 
     group_0 = WeightGather(0, 256, HEAD)
     group_1 = WeightGather(HEAD, HEAD + 256, 2 * HEAD)
-    group_g = WeightGather(GATE, COLS, COLS)
+    group_g = WeightGather(GATE, GATE + 384, COLS)
     group_0.start()
     gather_x.start()
     group_1.start()
@@ -338,13 +349,14 @@
 
     group_0.turn_b()
     gather_x.forward()
+    gather_d.start()
     group_0.turn_a()
     group_1.turn_b()
     group_1.turn_a()
+    group_g.turn_b()
     group_g.turn_a()
     own_x.wait()
     gather_x.finish()
-    gather_d.start()
 
     def norm_rows(block, carry):
         rows = pl.ds(pl.multiple_of(block * 128, 128), 128)
@@ -394,8 +406,8 @@
             att[rows, head * DH : (head + 1) * DH] = nn(weight, act[cols, cols_of(VALUE, head)])
 
     group_0.finish()
+    gather_d.forward()
     hidden_cols(0, HEAD)
-    gather_d.forward()
     group_1.share()
     forward(0)
     group_1.finish()
@@ -460,9 +472,26 @@
     )
     for head in range(2):
         cols = head_cols(head)
+        gated[:, cols] = ((att[:, cols] - att_mean) * att_inv * gate_of(head)).astype(BF16)
+
+    def out_block(k):
+        block = wg[at_y(k), :, :, :, WO:COLS].reshape(share, 2 * DH)
+        for half in range(2):
+            oterm[k, rows_of(half), :] = nt(gated[rows_of(half), :], block)
+
+    ring_o = RingSum(
+        links, lambda k, half: oterm[k, rows_of(half), :], yo_out, yo_in, dev_y(1), dev_y(3)
+    )
+    out_block(2)
+    ring_o.start_far()
+    out_block(1)
+    ring_o.start_right()
+    out_block(3)
+    ring_o.start_left()
+    for head in range(2):
+        cols = head_cols(head)
         att_norm = (att[:, cols] - att_mean) * att_inv
         gate = gate_of(head)
-        gated[:, cols] = (att_norm * gate).astype(BF16)
         g = gg[:, cols]
         here = slice(GATE + head * DH, GATE + (head + 1) * DH)
         gh[:, here] = (g * att_norm * slope[:, here]).astype(BF16)
@@ -549,11 +578,6 @@
     sum_e = WeightSum(GATE, COLS, COLS, bufs_e)
     sum_0 = WeightSum(0, 256, HEAD, bufs_0)
     sum_1 = WeightSum(HEAD, HEAD + 256, 2 * HEAD, bufs_1)
-
-    def out_block(k):
-        block = wg[at_y(k), :, :, :, WO:COLS].reshape(share, 2 * DH)
-        for half in range(2):
-            oterm[k, rows_of(half), :] = nt(gated[rows_of(half), :], block)
 
     def backward(head):
         mine_cols = head_cols(head)
@@ -579,20 +603,11 @@
         for half in range(2):
             iterm[k, rows_of(half), :] = nt(gh[rows_of(half), :], block)
 
-    ring_o = RingSum(
-        links, lambda k, half: oterm[k, rows_of(half), :], yo_out, yo_in, dev_y(1), dev_y(3)
-    )
     ring_i = RingSum(
         links, lambda k, half: iterm[k, rows_of(half), :], yi_out, yi_in, dev_y(1), dev_y(3)
     )
 
     sum_e.multiply([(dt, gated[...], WO), (xt, gh[:, GATE:WO], GATE)])
-    out_block(2)
-    ring_o.start_far()
-    out_block(1)
-    ring_o.start_right()
-    out_block(3)
-    ring_o.start_left()
     out_block(0)
     sum_e.join()
     backward(0)
@@ -628,6 +643,7 @@
     for half, value in enumerate(ring_o.finish()):
         rows = rows_of(half)
         output[rows, :] = (xg[y, rows, :].astype(F32) + value).astype(BF16)
+    write(0, output, output_hbm)
     sum_1.turn_b()
     sum_1.turn_a()
     stat2.arrived()
@@ -636,6 +652,7 @@
     row_avg, cross_avg = spread(sums2[0:1]), spread(sums2[1:2])
     gate_part, _ = sum_e.finish()
     grad_w_out[...] = gate_part[:, 256:512]
+    write(1, grad_w_out, grad_w_out_hbm)
     pieces = {GATE: gate_part[:, 0:128], GATE + DH: gate_part[:, 128:256]}
     for half, value in enumerate(ring_i.finish()):
         rows = rows_of(half)
@@ -647,6 +664,7 @@
             normed = (xg[y, rows, cols].astype(F32) - mean) * inverse
             centred = value[:, cols] - row_avg[here, lanes] - normed * cross_avg[here, lanes]
             grad_input[rows, cols] = dg[y, rows, cols].astype(F32) + centred * inverse
+    write(2, grad_input, grad_input_hbm)
     for head, group in enumerate((sum_0, sum_1)):
         low, high = group.finish()
         pieces[head * HEAD + QUERY] = low[:, 0:128]
@@ -657,18 +675,22 @@
         for part, place in enumerate(places):
             target = (head * 4 + part) * DH
             grad_w_in[:, target : target + DH] = pieces[place]
+    write(3, grad_w_in, grad_w_in_hbm)
     links.drain()
+    for copy in written:
+        copy.wait()
 
 
 def place_kernel(*refs):
-    sems = refs[-1]
-    count = len(refs) // 2
-    copies = [
-        pltpu.make_async_copy(refs[i], refs[count + i], sems.at[i]) for i in range(count)
-    ]
-    for copy in copies:
+    sources, targets, held, sems = refs[:4], refs[4:8], refs[8:12], refs[12]
+    inward = [pltpu.make_async_copy(sources[i], held[i], sems.at[i]) for i in range(4)]
+    outward = [pltpu.make_async_copy(held[i], targets[i], sems.at[4 + i]) for i in range(4)]
+    for copy in inward:
         copy.start()
-    for copy in copies:
+    for i in range(4):
+        inward[i].wait()
+        outward[i].start()
+    for copy in outward:
         copy.wait()
 
 
@@ -700,8 +722,12 @@
             whole,
             whole,
         ],
-        out_specs=[whole] * 4,
+        out_specs=[pl.BlockSpec(memory_space=pl.ANY)] * 4,
         scratch_shapes=[
+            vmem((tok, share), BF16),
+            vmem((tok, share), F32),
+            vmem(w_in.shape, F32),
+            vmem(w_out.shape[::-1], F32),
             vmem((NY, tok, share), BF16),
             vmem((NY, tok, share), BF16),
             vmem((tok, width), BF16),
@@ -740,7 +766,7 @@
             sum_bufs(256, 128),
             pltpu.SemaphoreType.DMA((N_SEM,)),
             pltpu.SemaphoreType.DMA((N_SEM,)),
-            pltpu.SemaphoreType.DMA((2,)),
+            pltpu.SemaphoreType.DMA((6,)),
         ],
         compiler_params=pltpu.CompilerParams(
             collective_id=0, has_side_effects=True, vmem_limit_bytes=60 * 1024 * 1024
@@ -752,7 +778,7 @@
         out_shape=[jax.ShapeDtypeStruct(r.shape, r.dtype) for r in results],
         in_specs=[anywhere] * 4,
         out_specs=[anywhere] * 4,
-        scratch_shapes=[pltpu.SemaphoreType.DMA((4,))],
+        scratch_shapes=[vmem(r.shape, r.dtype) for r in results] + [pltpu.SemaphoreType.DMA((8,))],
     )(*results)
     return output, grad_input, grad_w_in, grad_w_out.T
 

time: 87.1 us -> 60.3 us (0.69)
  Pallas kernels: 86.4 us -> 59.5 us
    pallas_call x1, Pallas kernels: 27.4 us -> 2 us  [shards(): pl.pallas_call(place_kernel, out_shape=[jax.ShapeDtypeStruct(r.shape, r.d...]
    pallas_call x1, Pallas kernels: 58.9 us -> 57.5 us  [shards(): pl.pallas_call(functools.partial(kernel, nz), out_shape=(jax.ShapeDtypeSt...]
where the time goes in v3:
time: 60.3 us; the launch traced here: 60.1 us
  Pallas kernels  59.5 us (99%)
  between operations  0.64 us (1%)
    pallas_call x1, Pallas kernels, shards(): pl.pallas_call(functools.partial(kernel, nz), out_shape=(jax.ShapeDtypeSt...  57.5 us
    pallas_call x1, Pallas kernels, shards(): pl.pallas_call(place_kernel, out_shape=[jax.ShapeDtypeStruct(r.shape, r.d...  2 us

profile of v3, /device:TPU:1, one launch (start us, length us, event | category | flops | bytes accessed | tf_op | source)
XLA Modules:
  0.0 60.1 jit_solution(6043661072460536751)
XLA Ops:
  0.6 57.5 %shard_map.84 = (bf16[512,256]{1,0:T(8,128)(2,1)}, f32[512,256]{1,0:T(8,128)}, f32[16,1024]{1,0:T(8,128)}, f32[16,256]{1,0:T(8,128)}) custom-call(bf16[512,256]{1,0:T(8,128)(2,1)} %history.1, bf16[512,256]{1,0:T(8,128)(2,1)} %out_grad.1, s32[1,8]{1,0:T(1,128)} %lengths.1, bf16[16,1024]{1,0:T(8,128)(2,1)} %w_in.1, bf16[16,256]{1,0:T(8,128)(2,1)} %bitcast.2), custom_call_target="tpu_custom_call" | custom-call | tf_op jit(solution)/shard_map/pallas_call | solution.py:710
  58.1 2.0 %shard_map.85 = (bf16[512,256]{1,0:T(8,128)(2,1)}, f32[512,256]{1,0:T(8,128)}, f32[16,1024]{1,0:T(8,128)}, f32[16,256]{1,0:T(8,128)}) custom-call(bf16[512,256]{1,0:T(8,128)(2,1)} %get-tuple-element.12.refs_0_, f32[512,256]{1,0:T(8,128)} %get-tuple-element.13.refs_1_, f32[16,1024]{1,0:T(8,128)} %get-tuple-element.14.refs_2_, f32[16,256]{1,0:T(8,128)} %get-tuple-element.15.refs_3_), custom_call_target="tpu_custom_call" | custom-call | tf_op jit(solution)/shard_map/pallas_call | solution.py:776

commit v4 on v3

--- a/solution.py
+++ b/solution.py
@@ -16,12 +16,11 @@
 BF16 = jnp.bfloat16
 NX = 4
 NY = 4
-N_SEM = 47
+N_SEM = 59
 
 HEAD = 3 * DH
 QUERY, KEY, VALUE = 0, DH, 2 * DH
 GATE, WO, COLS = 768, 1024, 1280
-Z_ORDER = (4, 3, 5, 2, 6, 1, 7)
 
 
 def nn(a, b):
@@ -38,14 +37,15 @@
 
 class Links:
     def __init__(self, send_sem, recv_sem):
-        self.send_sem, self.recv_sem, self.phases = send_sem, recv_sem, []
+        self.send_sem, self.recv_sem, self.phases, self.drained = send_sem, recv_sem, [], 0
 
     def phase(self, region):
         return Phase(self, region)
 
     def drain(self):
-        for phase in self.phases:
+        for phase in self.phases[self.drained :]:
             phase.sent()
+        self.drained = len(self.phases)
 
 
 class Phase:
@@ -142,13 +142,16 @@
     nz,
     history,
     out_grad,
-    lengths,
-    w_in,
-    w_out,
+    lengths_hbm,
+    w_in_hbm,
+    w_out_hbm,
     output_hbm,
     grad_input_hbm,
     grad_w_in_hbm,
     grad_w_out_hbm,
+    lengths,
+    w_in,
+    w_out,
     output,
     grad_input,
     grad_w_in,
@@ -179,13 +182,10 @@
     row_stat,
     st_own,
     st_in,
-    st2_own,
-    st2_in,
     yo_out,
     yo_in,
     yi_out,
     yi_in,
-    wsum,
     bufs_e,
     bufs_0,
     bufs_1,
@@ -203,25 +203,32 @@
     x = lax.div(me, 2 * nz)
     other = 1 - core
 
+    xs = [x] + [lax.rem(x + k, NX) for k in range(1, NX)]
+    zs = [z] + [lax.rem(z + k, nz) for k in range(1, nz)]
+    ys = [y] + [lax.rem(y + k, NY) for k in range(1, NY)]
+    x_devices = [((xx * nz + z) * 2 + core, y) for xx in xs]
+    z_devices = [((x * nz + zz) * 2 + core, y) for zz in zs]
+    y_devices = [(me, yy) for yy in ys]
+    sibling = ((x * nz + z) * 2 + other, y)
+
     def at_x(k):
-        return lax.rem(x + k, NX)
+        return xs[k % NX]
 
     def at_z(k):
-        return lax.rem(z + k, nz)
+        return zs[k % nz]
 
     def at_y(k):
-        return lax.rem(y + k, NY)
+        return ys[k % NY]
 
     def dev_x(k):
-        return {"dp": (at_x(k) * nz + z) * 2 + core}
+        return x_devices[k]
 
     def dev_z(k):
-        return {"dp": (x * nz + at_z(k)) * 2 + core}
+        return z_devices[k]
 
     def dev_y(k):
-        return {"inner": at_y(k)}
-
-    sibling = {"dp": (x * nz + z) * 2 + other}
+        return y_devices[k]
+
     links = Links(send_sem, recv_sem)
 
     written = []
@@ -241,10 +248,20 @@
     for device in partners:
         pl.semaphore_signal(barrier, inc=1, device_id=device, device_id_type=pl.DeviceIdType.MESH)
 
+    small = [
+        pltpu.make_async_copy(source, target, local_sem.at[6 + i])
+        for i, (source, target) in enumerate(
+            ((w_in_hbm, w_in), (w_out_hbm, w_out), (lengths_hbm, lengths))
+        )
+    ]
+    for copy in small:
+        copy.start()
     own_x = pltpu.make_async_copy(history, xg.at[y], local_sem.at[0])
     own_d = pltpu.make_async_copy(out_grad, dg.at[y], local_sem.at[1])
     own_x.start()
     own_d.start()
+    for copy in small:
+        copy.wait()
     mine = (x, z, core, slice(None))
     wg[mine + (slice(WO, COLS),)] = w_out[...]
     for head in range(2):
@@ -273,61 +290,77 @@
         lambda half: out_grad.at[rows_of(half)],
         dg.at[0],
     )
-    z_order = [k for k in Z_ORDER if k < nz] if nz == 8 else list(range(1, nz))
+    z_by_distance = sorted(range(1, nz), key=lambda k: min(k, nz - k))
+    z_near = [[k for k in z_by_distance if min(k, nz - k) <= 2]]
+    z_near += [[k for k in z_by_distance if min(k, nz - k) > 2]] if nz > 5 else []
+    z_far = [batch[::-1] for batch in z_near[::-1]]
+    z_order = z_by_distance[::-1]
     x_order = (2, 1, 3)
 
     class WeightGather:
         def __init__(self, first, middle, end):
+            self.all = pl.ds(first, end - first)
             self.ca = pl.ds(first, middle - first)
             self.cb = pl.ds(middle, end - middle) if end > middle else None
 
+        def to_x(self, zz):
+            piece = wg.at[x, zz, core, :, self.ca]
+            for k in x_order:
+                self.ax.send(piece, piece, dev_x(k))
+
+        def to_z(self, xx):
+            piece = wg.at[xx, z, core, :, self.cb]
+            for k in z_order:
+                self.bz.send(piece, piece, dev_z(k))
+
         def start(self):
+            own_a = wg.at[x, z, core, :, self.ca]
+            self.ax = links.phase(wg.at[0 : NX - 1, :, core, :, self.ca])
+            self.az = []
+            for batch in z_near:
+                self.az.append(links.phase(wg.at[x, 0 : len(batch), core, :, self.ca]))
+                for k in batch:
+                    self.az[-1].send(own_a, own_a, dev_z(k))
             if self.cb:
-                own = wg.at[x, z, core, :, self.cb]
+                own_b = wg.at[x, z, core, :, self.cb]
+                self.bz = links.phase(wg.at[:, 0 : nz - 1, core, :, self.cb])
                 self.bx = links.phase(wg.at[0 : NX - 1, z, core, :, self.cb])
                 for k in x_order:
-                    self.bx.send(own, own, dev_x(k))
-            own = wg.at[x, z, core, :, self.ca]
-            self.az = links.phase(wg.at[x, 0 : nz - 1, core, :, self.ca])
-            for k in z_order:
-                self.az.send(own, own, dev_z(k))
+                    self.bx.send(own_b, own_b, dev_x(k))
+            self.to_x(z)
+            if self.cb:
+                self.to_z(x)
 
         def turn_b(self):
             if self.cb:
                 self.bx.arrived()
-                slab = wg.at[:, z, core, :, self.cb]
-                self.bz = links.phase(wg.at[:, 0 : nz - 1, core, :, self.cb])
-                for k in z_order:
-                    self.bz.send(slab, slab, dev_z(k))
-
-        def turn_a(self):
-            self.az.arrived()
-            slab = wg.at[x, :, core, :, self.ca]
-            self.ax = links.phase(wg.at[0 : NX - 1, :, core, :, self.ca])
-            for k in x_order:
-                self.ax.send(slab, slab, dev_x(k))
+                for k in x_order:
+                    self.to_z(at_x(NX - k))
+
+        def turn_a(self, *indices):
+            for index in indices:
+                self.az[index].arrived()
+                for k in z_near[index]:
+                    self.to_x(at_z(nz - k))
 
         def share(self):
-            self.shared = []
-            for last, cols in ((self.bz if self.cb else None, self.cb), (self.ax, self.ca)):
-                if cols is not None:
-                    last.arrived()
-                    region = wg.at[:, :, core, :, cols]
-                    phase = links.phase(region)
-                    phase.send(region, region, sibling)
-                    self.shared.append(phase)
+            if self.cb:
+                self.bz.arrived()
+            self.ax.arrived()
+            region = wg.at[:, :, core, :, self.all]
+            self.shared = links.phase(region)
+            self.shared.send(region, region, sibling)
 
         def finish(self):
-            for phase in self.shared:
-                phase.arrived()
+            self.shared.arrived()
 
     group_0 = WeightGather(0, 256, HEAD)
     group_1 = WeightGather(HEAD, HEAD + 256, 2 * HEAD)
     group_g = WeightGather(GATE, GATE + 384, COLS)
     group_0.start()
-    gather_x.start()
     group_1.start()
     group_g.start()
+    gather_x.start()
 
     blocks = tok // 128
     ends = []
@@ -347,14 +380,16 @@
                 allowed, 1.0 / MAXLEN, 0.0
             ).astype(F32)
 
+    far = len(z_near) - 1
     group_0.turn_b()
+    group_0.turn_a(0)
     gather_x.forward()
     gather_d.start()
-    group_0.turn_a()
+    group_0.turn_a(*range(1, far + 1))
     group_1.turn_b()
-    group_1.turn_a()
+    group_1.turn_a(*range(far + 1))
     group_g.turn_b()
-    group_g.turn_a()
+    group_g.turn_a(*range(far + 1))
     own_x.wait()
     gather_x.finish()
 
@@ -371,6 +406,9 @@
         return carry
 
     lax.fori_loop(0, blocks, norm_rows, 0)
+    gather_d.forward()
+    for k in range(NY):
+        xt[k] = xh[:, k * share : (k + 1) * share].T.reshape(nz, 2, 16, tok)
     group_0.share()
 
     def weight_cols(first, count):
@@ -406,7 +444,6 @@
             att[rows, head * DH : (head + 1) * DH] = nn(weight, act[cols, cols_of(VALUE, head)])
 
     group_0.finish()
-    gather_d.forward()
     hidden_cols(0, HEAD)
     group_1.share()
     forward(0)
@@ -414,10 +451,45 @@
     hidden_cols(HEAD, HEAD)
     group_g.share()
     forward(1)
+
+    def columns_sum(value):
+        return jnp.sum(value.T, 0, keepdims=True)
+
+    def head_cols(head):
+        return slice(head * DH, (head + 1) * DH)
+
+    def gate_of(head):
+        return act[:, GATE + head * DH : GATE + (head + 1) * DH].astype(F32)
+
+    def spread(row_values):
+        return jnp.broadcast_to(row_values, (128, tok)).T
+
+    class RowSums:
+        def __init__(self, own, inn):
+            self.own, self.inn = own, inn
+
+        def start(self, first, second):
+            self.own[0:1, :] = columns_sum(first)
+            self.own[1:2, :] = columns_sum(second)
+            self.phase = links.phase(self.inn.at[0 : NY - 1])
+            for k in x_order:
+                self.phase.send(self.own, self.inn.at[y], dev_y(k))
+
+        def finish(self):
+            self.phase.arrived()
+            self.inn[y] = self.own[...]
+            sums = self.inn[0] + self.inn[1] + self.inn[2] + self.inn[3]
+            return sums[0:1] / width, sums[1:2] / width
+
+    att_sums = RowSums(st_own.at[0], st_in.at[0])
+    norm_sums = RowSums(st_own.at[1], st_in.at[1])
+    input_sums = RowSums(st_own.at[2], st_in.at[2])
+    low, high = att[:, 0:DH], att[:, DH : 2 * DH]
+    att_sums.start(low + high, low * low + high * high)
+    group_g.finish()
+    hidden_cols(GATE, 2 * DH)
     own_d.wait()
     gather_d.finish()
-    group_g.finish()
-    hidden_cols(GATE, 2 * DH)
     for half in range(2):
         rows = rows_of(half)
         total_gg = None
@@ -426,53 +498,23 @@
             piece = nn(dg[k, rows, :], block)
             total_gg = piece if total_gg is None else total_gg + piece
         gg[rows, :] = total_gg
-
-    def columns_sum(value):
-        return jnp.sum(value.T, 0, keepdims=True)
-
-    def gate_of(head):
-        return act[:, GATE + head * DH : GATE + (head + 1) * DH].astype(F32)
-
-    def head_cols(head):
-        return slice(head * DH, (head + 1) * DH)
-
-    sums = [0.0] * 4
+    plain, cross = 0.0, 0.0
     for head in range(2):
-        a = att[:, head_cols(head)]
         g = gg[:, head_cols(head)] * gate_of(head)
-        for k, term_k in enumerate((a, a * a, g, g * a)):
-            sums[k] = sums[k] + term_k
-    for k in range(4):
-        st_own[k : k + 1, :] = columns_sum(sums[k])
-    stat = links.phase(st_in.at[0 : NY - 1])
-    for k in x_order:
-        stat.send(st_own, st_in.at[y], dev_y(k))
+        plain = plain + g
+        cross = cross + g * att[:, head_cols(head)]
+    norm_sums.start(plain, cross)
     for k in range(NY):
-        cols = slice(k * share, (k + 1) * share)
-        xt[k] = xh[:, cols].T.reshape(nz, 2, 16, tok)
         dt[k] = dg[k].T.reshape(nz, 2, 16, tok)
-    w_sum = jnp.zeros((1, WO), F32)
-    for k in range(NX):
-        block = wg[k, :, :, :, 0:WO].reshape(share, WO).astype(F32)
-        w_sum = w_sum + jnp.sum(block, 0, keepdims=True)
-    wsum[...] = w_sum
-    stat.arrived()
-    st_in[y] = st_own[...]
-    sums = st_in[0] + st_in[1] + st_in[2] + st_in[3]
-
-    def spread(row_values):
-        return jnp.broadcast_to(row_values, (128, tok)).T
-
-    att_mean = sums[0:1] / (H * DH)
-    att_inv = lax.rsqrt(sums[1:2] / (H * DH) - att_mean * att_mean + EPSILON)
-    norm_mean = sums[2:3] / (H * DH)
-    cross_mean = (sums[3:4] - att_mean * sums[2:3]) * att_inv / (H * DH)
-    att_mean, att_inv, norm_mean, cross_mean = (
-        spread(value) for value in (att_mean, att_inv, norm_mean, cross_mean)
-    )
+
+    mean_row, square_row = att_sums.finish()
+    inv_row = lax.rsqrt(square_row - mean_row * mean_row + EPSILON)
+    att_mean, att_inv = spread(mean_row), spread(inv_row)
     for head in range(2):
         cols = head_cols(head)
-        gated[:, cols] = ((att[:, cols] - att_mean) * att_inv * gate_of(head)).astype(BF16)
+        att_norm = (att[:, cols] - att_mean) * att_inv
+        att[:, cols] = att_norm
+        gated[:, cols] = (att_norm * gate_of(head)).astype(BF16)
 
     def out_block(k):
         block = wg[at_y(k), :, :, :, WO:COLS].reshape(share, 2 * DH)
@@ -484,102 +526,96 @@
     )
     out_block(2)
     ring_o.start_far()
-    out_block(1)
-    ring_o.start_right()
-    out_block(3)
-    ring_o.start_left()
     for head in range(2):
-        cols = head_cols(head)
-        att_norm = (att[:, cols] - att_mean) * att_inv
-        gate = gate_of(head)
-        g = gg[:, cols]
         here = slice(GATE + head * DH, GATE + (head + 1) * DH)
-        gh[:, here] = (g * att_norm * slope[:, here]).astype(BF16)
-        ga[:, cols] = ((g * gate - norm_mean - att_norm * cross_mean) * att_inv).astype(BF16)
+        gh[:, here] = (gg[:, head_cols(head)] * att[:, head_cols(head)] * slope[:, here]).astype(BF16)
 
     class WeightSum:
         def __init__(self, first, middle, end, bufs):
             self.a, self.b = slice(first, middle), slice(middle, end)
             self.all = slice(first, end)
             self.ax, self.az = bufs[0], bufs[1]
-            self.bz, self.bx = bufs[2:4] if end > middle else (None, None)
-
-        def multiply(self, products):
+            self.bz, self.bx = bufs[2], bufs[3]
+
+        def multiply(self, products, own):
             everything = (slice(None), slice(None), slice(None))
-            view = everything + (self.all,)
-            for parity, own in ((other, False), (core, True)):
-                for lhs, rhs, first in products:
-                    count = rhs.shape[1]
-                    here = everything + (slice(first, first + count),)
-                    rows = lhs[:, :, parity].reshape(width // 2, tok)
-                    value = nn(rows, rhs).reshape(NX, nz, 16, count)
-                    if own:
-                        term[here] = value
-                    else:
-                        sib_out[here] = value.astype(BF16)
-                if not own:
-                    self.pair = links.phase(sib_in.at[view])
-                    self.pair.send(sib_out.at[view], sib_in.at[view], sibling)
+            for lhs, rhs, first in products:
+                count = rhs.shape[1]
+                here = everything + (slice(first, first + count),)
+                rows = lhs[:, :, core if own else other].reshape(width // 2, tok)
+                value = nn(rows, rhs).reshape(NX, nz, 16, count)
+                if own:
+                    term[here] = value
+                else:
+                    sib_out[here] = value.astype(BF16)
+            if not own:
+                view = everything + (self.all,)
+                self.pair = links.phase(sib_in.at[view])
+                self.pair.send(sib_out.at[view], sib_in.at[view], sibling)
 
         def joined(self, place):
             return term[place] + sib_in[place].astype(F32)
 
         def join(self):
             self.pair.arrived()
-            if self.bz is not None:
-                self.pz = links.phase(self.bz.at[0])
-                for k in z_order:
-                    self.bz[0, k - 1] = self.joined((slice(None), at_z(k), slice(None), self.b)).astype(BF16)
-                    self.pz.send(self.bz.at[0, k - 1], self.bz.at[1, k - 1], dev_z(k))
-            self.px = links.phase(self.ax.at[0])
-            for k in x_order:
-                self.ax[0, k - 1] = self.joined((at_x(k), slice(None), slice(None), self.a)).astype(BF16)
-                self.px.send(self.ax.at[0, k - 1], self.ax.at[1, k - 1], dev_x(k))
+            self.px, self.pz = [], []
+            for batch in z_far + [(0,)]:
+                self.px.append(links.phase(self.ax.at[0, 0 : len(batch)]))
+                for j in batch:
+                    for k in x_order:
+                        place = (at_x(k), at_z(j), slice(None), self.a)
+                        self.ax[0, j, k - 1] = self.joined(place).astype(BF16)
+                        self.px[-1].send(self.ax.at[0, j, k - 1], self.ax.at[1, j, k - 1], dev_x(k))
+            for batch in (x_order, (0,)):
+                self.pz.append(links.phase(self.bz.at[0, 0 : len(batch)]))
+                for j in batch:
+                    for k in z_order:
+                        place = (at_x(j), at_z(k), slice(None), self.b)
+                        self.bz[0, j, k - 1] = self.joined(place).astype(BF16)
+                        self.pz[-1].send(self.bz.at[0, j, k - 1], self.bz.at[1, j, k - 1], dev_z(k))
+            self.pza, self.pxb = links.phase(self.az.at[0]), links.phase(self.bx.at[0])
 
         def turn_b(self):
-            if self.bz is None:
-                return
-            place = (slice(None), z, slice(None), self.b)
-            value = self.joined(place)
-            self.pz.arrived()
-            for k in range(nz - 1):
-                value = value + self.bz[1, k].astype(F32)
-            term[place] = value
-            self.pxb = links.phase(self.bx.at[0])
-            for k in x_order:
-                self.bx[0, k - 1] = term[at_x(k), z, :, self.b].astype(BF16)
-                self.pxb.send(self.bx.at[0, k - 1], self.bx.at[1, k - 1], dev_x(k))
+            for batch, phase in zip((x_order, (0,)), self.pz):
+                phase.arrived()
+                for j in batch:
+                    value = self.joined((at_x(j), z, slice(None), self.b))
+                    for k in range(nz - 1):
+                        value = value + self.bz[1, j, k].astype(F32)
+                    if j:
+                        self.bx[0, j - 1] = value.astype(BF16)
+                        self.pxb.send(self.bx.at[0, j - 1], self.bx.at[1, j - 1], dev_x(j))
+                    else:
+                        self.own_b = value
 
         def turn_a(self):
-            place = (x, slice(None), slice(None), self.a)
-            value = self.joined(place)
-            self.px.arrived()
-            for k in range(NX - 1):
-                value = value + self.ax[1, k].astype(F32)
-            term[place] = value
-            self.pza = links.phase(self.az.at[0])
-            for k in z_order:
-                self.az[0, k - 1] = term[x, at_z(k), :, self.a].astype(BF16)
-                self.pza.send(self.az.at[0, k - 1], self.az.at[1, k - 1], dev_z(k))
+            for batch, phase in zip(z_far + [(0,)], self.px):
+                phase.arrived()
+                for j in batch:
+                    value = self.joined((x, at_z(j), slice(None), self.a))
+                    for k in range(NX - 1):
+                        value = value + self.ax[1, j, k].astype(F32)
+                    if j:
+                        self.az[0, j - 1] = value.astype(BF16)
+                        self.pza.send(self.az.at[0, j - 1], self.az.at[1, j - 1], dev_z(j))
+                    else:
+                        self.own_a = value
 
         def finish(self):
-            value_a = term[x, z, :, self.a]
+            value_a, value_b = self.own_a, self.own_b
             self.pza.arrived()
             for k in range(nz - 1):
                 value_a = value_a + self.az[1, k].astype(F32)
-            if self.bz is None:
-                return value_a, None
-            value_b = term[x, z, :, self.b]
             self.pxb.arrived()
             for k in range(NX - 1):
                 value_b = value_b + self.bx[1, k].astype(F32)
             return value_a, value_b
 
-    sum_e = WeightSum(GATE, COLS, COLS, bufs_e)
+    sum_e = WeightSum(GATE, GATE + 384, COLS, bufs_e)
     sum_0 = WeightSum(0, 256, HEAD, bufs_0)
     sum_1 = WeightSum(HEAD, HEAD + 256, 2 * HEAD, bufs_1)
 
-    def backward(head):
+    def backward_rows(head):
         mine_cols = head_cols(head)
         for i in range(blocks):
             rows, cols = band(i)
@@ -589,6 +625,9 @@
             grad_q = SCALE * nn(grad_score, act[cols, cols_of(KEY, head)])
             here = cols_of(QUERY, head)
             gh[rows, here] = (grad_q * slope[rows, here]).astype(BF16)
+
+    def backward_cols(head):
+        mine_cols = head_cols(head)
         for j in range(blocks):
             cols = slice(j * 128, (j + 1) * 128)
             rows = slice(j * 128, min(j + 3, blocks) * 128)
@@ -607,51 +646,67 @@
         links, lambda k, half: iterm[k, rows_of(half), :], yi_out, yi_in, dev_y(1), dev_y(3)
     )
 
-    sum_e.multiply([(dt, gated[...], WO), (xt, gh[:, GATE:WO], GATE)])
-    out_block(0)
+    early = [(dt, gated[...], WO), (xt, gh[:, GATE:WO], GATE)]
+    sum_e.multiply(early, False)
+    out_block(1)
+    ring_o.start_right()
+    sum_e.multiply(early, True)
+    out_block(3)
+    ring_o.start_left()
     sum_e.join()
-    backward(0)
-    sum_0.multiply([(xt, gh[:, 0:HEAD], 0)])
+    norm_mean, cross_row = norm_sums.finish()
+    cross_mean = spread((cross_row - mean_row * norm_mean) * inv_row)
+    norm_mean = spread(norm_mean)
+    for head in range(2):
+        cols = head_cols(head)
+        grad_norm = gg[:, cols] * gate_of(head)
+        ga[:, cols] = ((grad_norm - norm_mean - att[:, cols] * cross_mean) * att_inv).astype(BF16)
+    backward_rows(0)
+    backward_cols(0)
+    sum_0.multiply([(xt, gh[:, 0:HEAD], 0)], False)
+    sum_0.multiply([(xt, gh[:, 0:HEAD], 0)], True)
     ring_o.middle()
+    backward_rows(1)
     sum_0.join()
-    backward(1)
-    sum_1.multiply([(xt, gh[:, HEAD : 2 * HEAD], HEAD)])
+    backward_cols(1)
+    sum_1.multiply([(xt, gh[:, HEAD : 2 * HEAD], HEAD)], False)
     in_block(2)
     ring_i.start_far()
+    sum_1.multiply([(xt, gh[:, HEAD : 2 * HEAD], HEAD)], True)
     sum_1.join()
     in_block(1)
     ring_i.start_right()
     in_block(3)
     ring_i.start_left()
     in_block(0)
+    sum_e.turn_b()
     sum_e.turn_a()
-
+    sum_0.turn_b()
+    sum_0.turn_a()
+    ring_i.middle()
+    sum_1.turn_b()
+    sum_1.turn_a()
+
+    w_sum = jnp.zeros((1, WO), F32)
+    for k in range(NX):
+        block = wg[k, :, :, :, 0:WO].reshape(share, WO).astype(F32)
+        w_sum = w_sum + jnp.sum(block, 0, keepdims=True)
     plain, cross = 0.0, 0.0
     for k in range(WO // 128):
         cols = slice(k * 128, (k + 1) * 128)
         piece = gh[:, cols].astype(F32)
-        plain = plain + piece * wsum[:, cols]
+        plain = plain + piece * w_sum[:, cols]
         cross = cross + piece * hid[:, cols]
-    st2_own[0:1, :] = columns_sum(plain)
-    st2_own[1:2, :] = columns_sum(cross)
-    stat2 = links.phase(st2_in.at[0 : NY - 1])
-    for k in x_order:
-        stat2.send(st2_own, st2_in.at[y], dev_y(k))
-    sum_0.turn_b()
-    sum_0.turn_a()
-    ring_i.middle()
+    input_sums.start(plain, cross)
+    out_block(0)
     for half, value in enumerate(ring_o.finish()):
         rows = rows_of(half)
         output[rows, :] = (xg[y, rows, :].astype(F32) + value).astype(BF16)
     write(0, output, output_hbm)
-    sum_1.turn_b()
-    sum_1.turn_a()
-    stat2.arrived()
-    st2_in[y] = st2_own[...]
-    sums2 = (st2_in[0] + st2_in[1] + st2_in[2] + st2_in[3]) / width
-    row_avg, cross_avg = spread(sums2[0:1]), spread(sums2[1:2])
-    gate_part, _ = sum_e.finish()
-    grad_w_out[...] = gate_part[:, 256:512]
+    row_avg, cross_avg = (spread(row) for row in input_sums.finish())
+    gate_part, out_part = sum_e.finish()
+    grad_w_out[:, 0:128] = gate_part[:, 256:384]
+    grad_w_out[:, 128:256] = out_part
     write(1, grad_w_out, grad_w_out_hbm)
     pieces = {GATE: gate_part[:, 0:128], GATE + DH: gate_part[:, 128:256]}
     for half, value in enumerate(ring_i.finish()):
@@ -701,12 +756,13 @@
     cols = WO
     vmem = pltpu.VMEM
     def sum_bufs(wa, wb):
-        out = [vmem((2, NX - 1, nz, 16, wa), BF16), vmem((2, nz - 1, 16, wa), BF16)]
-        if wb:
-            out += [vmem((2, nz - 1, NX, 16, wb), BF16), vmem((2, NX - 1, 16, wb), BF16)]
-        return out
-
-    whole = pl.BlockSpec(memory_space=pltpu.VMEM)
+        return [
+            vmem((2, nz, NX - 1, 16, wa), BF16),
+            vmem((2, nz - 1, 16, wa), BF16),
+            vmem((2, NX, nz - 1, 16, wb), BF16),
+            vmem((2, NX - 1, 16, wb), BF16),
+        ]
+
     results = pl.pallas_call(
         functools.partial(kernel, nz),
         out_shape=(
@@ -717,13 +773,13 @@
         ),
         in_specs=[
             pl.BlockSpec(memory_space=pl.ANY),
-            pl.BlockSpec(memory_space=pl.ANY),
-            pl.BlockSpec(memory_space=pltpu.SMEM),
-            whole,
-            whole,
-        ],
+        ]
+        * 5,
         out_specs=[pl.BlockSpec(memory_space=pl.ANY)] * 4,
         scratch_shapes=[
+            pltpu.SMEM(lengths.shape, lengths.dtype),
+            vmem(w_in.shape, BF16),
+            vmem(w_out.shape[::-1], BF16),
             vmem((tok, share), BF16),
             vmem((tok, share), F32),
             vmem(w_in.shape, F32),
@@ -752,21 +808,18 @@
             vmem((NY, tok, share), F32),
             vmem((NY, tok, share), F32),
             vmem((2, tok, 128), F32),
-            vmem((8, tok), F32),
-            vmem((NY, 8, tok), F32),
-            vmem((8, tok), F32),
-            vmem((NY, 8, tok), F32),
+            vmem((3, 8, tok), F32),
+            vmem((3, NY, 8, tok), F32),
             vmem((6, half, share), BF16),
             vmem((6, half, share), BF16),
             vmem((6, half, share), BF16),
             vmem((6, half, share), BF16),
-            vmem((1, WO), F32),
-            sum_bufs(512, 0),
+            sum_bufs(384, 128),
             sum_bufs(256, 128),
             sum_bufs(256, 128),
             pltpu.SemaphoreType.DMA((N_SEM,)),
             pltpu.SemaphoreType.DMA((N_SEM,)),
-            pltpu.SemaphoreType.DMA((6,)),
+            pltpu.SemaphoreType.DMA((9,)),
         ],
         compiler_params=pltpu.CompilerParams(
             collective_id=0, has_side_effects=True, vmem_limit_bytes=60 * 1024 * 1024

time: 60.3 us -> 59.1 us (0.980)
  Pallas kernels: 59.5 us -> 58.4 us
    pallas_call x1, Pallas kernels: 57.5 us -> 56.4 us  [shards(): pl.pallas_call(functools.partial(kernel, nz), out_shape=(jax.ShapeDtypeSt...]
where the time goes in v4:
time: 59.1 us; the launch traced here: 59 us
  Pallas kernels  58.4 us (99%)
  between operations  0.64 us (1%)
    pallas_call x1, Pallas kernels, shards(): pl.pallas_call(functools.partial(kernel, nz), out_shape=(jax.ShapeDtypeSt...  56.4 us
    pallas_call x1, Pallas kernels, shards(): pl.pallas_call(place_kernel, out_shape=[jax.ShapeDtypeStruct(r.shape, r.d...  2 us

profile of v4, /device:TPU:1, one launch (start us, length us, event | category | flops | bytes accessed | tf_op | source)
XLA Modules:
  0.0 59.0 jit_solution(11980623857504383818)
XLA Ops:
  0.6 56.4 %shard_map.84 = (bf16[512,256]{1,0:T(8,128)(2,1)}, f32[512,256]{1,0:T(8,128)}, f32[16,1024]{1,0:T(8,128)}, f32[16,256]{1,0:T(8,128)}) custom-call(bf16[512,256]{1,0:T(8,128)(2,1)} %history.1, bf16[512,256]{1,0:T(8,128)(2,1)} %out_grad.1, s32[1,8]{1,0:T(1,128)} %lengths_hbm.1, bf16[16,1024]{1,0:T(8,128)(2,1)} %w_in_hbm.1, bf16[16,256]{1,0:T(8,128)(2,1)} %bitcast.2), custom_call_target="tpu_custom_call" | custom-call | tf_op jit(solution)/shard_map/pallas_call | solution.py:766
  57.0 2.0 %shard_map.85 = (bf16[512,256]{1,0:T(8,128)(2,1)}, f32[512,256]{1,0:T(8,128)}, f32[16,1024]{1,0:T(8,128)}, f32[16,256]{1,0:T(8,128)}) custom-call(bf16[512,256]{1,0:T(8,128)(2,1)} %get-tuple-element.12.refs_0_, f32[512,256]{1,0:T(8,128)} %get-tuple-element.13.refs_1_, f32[16,1024]{1,0:T(8,128)} %get-tuple-element.14.refs_2_, f32[16,256]{1,0:T(8,128)} %get-tuple-element.15.refs_3_), custom_call_target="tpu_custom_call" | custom-call | tf_op jit(solution)/shard_map/pallas_call | solution.py:829

commit v5 on v4

--- a/solution.py
+++ b/solution.py
@@ -104,7 +104,8 @@
 
 
 class RingSum:
-    def __init__(self, links, part, out_buf, in_buf, right, left):
+    def __init__(self, links, make, part, out_buf, in_buf, right, left):
+        self.make = make
         self.links, self.part, self.out, self.inn = links, part, out_buf, in_buf
         self.right, self.left = right, left
 
@@ -116,13 +117,17 @@
         links = self.links
         self.p0, self.p1 = links.phase(self.out.at[0]), links.phase(self.out.at[1])
         self.rest = links.phase(self.out.at[2:6])
+        self.make(2, (0,))
         self.push(self.p0, 0, self.part(2, 0), self.right)
+        self.make(2, (1,))
         self.push(self.p1, 1, self.part(2, 1), self.left)
 
     def start_right(self):
+        self.make(1, (1, 0))
         self.push(self.rest, 2, self.part(1, 1), self.right)
 
     def start_left(self):
+        self.make(3, (0, 1))
         self.push(self.rest, 3, self.part(3, 0), self.left)
 
     def middle(self):
@@ -240,10 +245,10 @@
 
     barrier = pltpu.get_barrier_semaphore()
     partners = (
-        [sibling]
-        + [dev_y(k) for k in (1, 2, 3)]
-        + [dev_x(k) for k in (1, 2, 3)]
-        + [dev_z(k) for k in range(1, nz)]
+        [dev_z(k) for k in sorted(range(1, nz), key=lambda k: -min(k, nz - k))]
+        + [dev_x(k) for k in (2, 1, 3)]
+        + [dev_y(k) for k in (2, 1, 3)]
+        + [sibling]
     )
     for device in partners:
         pl.semaphore_signal(barrier, inc=1, device_id=device, device_id_type=pl.DeviceIdType.MESH)
@@ -359,7 +364,6 @@
     group_g = WeightGather(GATE, GATE + 384, COLS)
     group_0.start()
     group_1.start()
-    group_g.start()
     gather_x.start()
 
     blocks = tok // 128
@@ -383,6 +387,7 @@
     far = len(z_near) - 1
     group_0.turn_b()
     group_0.turn_a(0)
+    group_g.start()
     gather_x.forward()
     gather_d.start()
     group_0.turn_a(*range(1, far + 1))
@@ -405,11 +410,11 @@
             xh[rows, k * share : (k + 1) * share] = ((cols[k] - mean) * inverse).astype(BF16)
         return carry
 
+    gather_d.forward()
+    group_0.share()
     lax.fori_loop(0, blocks, norm_rows, 0)
-    gather_d.forward()
     for k in range(NY):
         xt[k] = xh[:, k * share : (k + 1) * share].T.reshape(nz, 2, 16, tok)
-    group_0.share()
 
     def weight_cols(first, count):
         return wg[:, :, :, :, first : first + count].reshape(width, count)
@@ -516,15 +521,14 @@
         att[:, cols] = att_norm
         gated[:, cols] = (att_norm * gate_of(head)).astype(BF16)
 
-    def out_block(k):
+    def out_block(k, halves=(0, 1)):
         block = wg[at_y(k), :, :, :, WO:COLS].reshape(share, 2 * DH)
-        for half in range(2):
+        for half in halves:
             oterm[k, rows_of(half), :] = nt(gated[rows_of(half), :], block)
 
     ring_o = RingSum(
-        links, lambda k, half: oterm[k, rows_of(half), :], yo_out, yo_in, dev_y(1), dev_y(3)
+        links, out_block, lambda k, half: oterm[k, rows_of(half), :], yo_out, yo_in, dev_y(1), dev_y(3)
     )
-    out_block(2)
     ring_o.start_far()
     for head in range(2):
         here = slice(GATE + head * DH, GATE + (head + 1) * DH)
@@ -637,21 +641,19 @@
                 here = cols_of(base, head)
                 gh[cols, here] = (value * slope[cols, here]).astype(BF16)
 
-    def in_block(k):
+    def in_block(k, halves=(0, 1)):
         block = wg[at_y(k), :, :, :, 0:WO].reshape(share, WO)
-        for half in range(2):
+        for half in halves:
             iterm[k, rows_of(half), :] = nt(gh[rows_of(half), :], block)
 
     ring_i = RingSum(
-        links, lambda k, half: iterm[k, rows_of(half), :], yi_out, yi_in, dev_y(1), dev_y(3)
+        links, in_block, lambda k, half: iterm[k, rows_of(half), :], yi_out, yi_in, dev_y(1), dev_y(3)
     )
 
     early = [(dt, gated[...], WO), (xt, gh[:, GATE:WO], GATE)]
     sum_e.multiply(early, False)
-    out_block(1)
     ring_o.start_right()
     sum_e.multiply(early, True)
-    out_block(3)
     ring_o.start_left()
     sum_e.join()
     norm_mean, cross_row = norm_sums.finish()
@@ -670,13 +672,10 @@
     sum_0.join()
     backward_cols(1)
     sum_1.multiply([(xt, gh[:, HEAD : 2 * HEAD], HEAD)], False)
-    in_block(2)
     ring_i.start_far()
     sum_1.multiply([(xt, gh[:, HEAD : 2 * HEAD], HEAD)], True)
     sum_1.join()
-    in_block(1)
     ring_i.start_right()
-    in_block(3)
     ring_i.start_left()
     in_block(0)
     sum_e.turn_b()

time: 59.1 us -> 58.5 us (0.990)
  Pallas kernels: 58.4 us -> 57.8 us
where the time goes in v5:
time: 58.5 us; the launch traced here: 58.4 us
  Pallas kernels  57.8 us (99%)
  between operations  0.64 us (1%)
    pallas_call x1, Pallas kernels, shards(): pl.pallas_call(functools.partial(kernel, nz), out_shape=(jax.ShapeDtypeSt...  55.8 us
    pallas_call x1, Pallas kernels, shards(): pl.pallas_call(place_kernel, out_shape=[jax.ShapeDtypeStruct(r.shape, r.d...  2 us

profile of v5, /device:TPU:1, one launch (start us, length us, event | category | flops | bytes accessed | tf_op | source)
XLA Modules:
  0.0 58.4 jit_solution(4483034632062887557)
XLA Ops:
  0.6 55.8 %shard_map.84 = (bf16[512,256]{1,0:T(8,128)(2,1)}, f32[512,256]{1,0:T(8,128)}, f32[16,1024]{1,0:T(8,128)}, f32[16,256]{1,0:T(8,128)}) custom-call(bf16[512,256]{1,0:T(8,128)(2,1)} %history.1, bf16[512,256]{1,0:T(8,128)(2,1)} %out_grad.1, s32[1,8]{1,0:T(1,128)} %lengths_hbm.1, bf16[16,1024]{1,0:T(8,128)(2,1)} %w_in_hbm.1, bf16[16,256]{1,0:T(8,128)(2,1)} %bitcast.2), custom_call_target="tpu_custom_call" | custom-call | tf_op jit(solution)/shard_map/pallas_call | solution.py:765
  56.4 2.0 %shard_map.85 = (bf16[512,256]{1,0:T(8,128)(2,1)}, f32[512,256]{1,0:T(8,128)}, f32[16,1024]{1,0:T(8,128)}, f32[16,256]{1,0:T(8,128)}) custom-call(bf16[512,256]{1,0:T(8,128)(2,1)} %get-tuple-element.12.refs_0_, f32[512,256]{1,0:T(8,128)} %get-tuple-element.13.refs_1_, f32[16,1024]{1,0:T(8,128)} %get-tuple-element.14.refs_2_, f32[16,256]{1,0:T(8,128)} %get-tuple-element.15.refs_3_), custom_call_target="tpu_custom_call" | custom-call | tf_op jit(solution)/shard_map/pallas_call | solution.py:828

commit v6 on v5

--- a/solution.py
+++ b/solution.py
@@ -16,7 +16,7 @@
 BF16 = jnp.bfloat16
 NX = 4
 NY = 4
-N_SEM = 59
+N_SEM = 57
 
 HEAD = 3 * DH
 QUERY, KEY, VALUE = 0, DH, 2 * DH
@@ -42,10 +42,11 @@
     def phase(self, region):
         return Phase(self, region)
 
-    def drain(self):
-        for phase in self.phases[self.drained :]:
+    def drain(self, count=None):
+        count = len(self.phases) if count is None else count
+        for phase in self.phases[self.drained : count]:
             phase.sent()
-        self.drained = len(self.phases)
+        self.drained = count
 
 
 class Phase:
@@ -361,7 +362,7 @@
 
     group_0 = WeightGather(0, 256, HEAD)
     group_1 = WeightGather(HEAD, HEAD + 256, 2 * HEAD)
-    group_g = WeightGather(GATE, GATE + 384, COLS)
+    group_g = WeightGather(GATE, COLS, COLS)
     group_0.start()
     group_1.start()
     gather_x.start()
@@ -490,6 +491,7 @@
     norm_sums = RowSums(st_own.at[1], st_in.at[1])
     input_sums = RowSums(st_own.at[2], st_in.at[2])
     low, high = att[:, 0:DH], att[:, DH : 2 * DH]
+    gathered = len(links.phases)
     att_sums.start(low + high, low * low + high * high)
     group_g.finish()
     hidden_cols(GATE, 2 * DH)
@@ -656,6 +658,7 @@
     sum_e.multiply(early, True)
     ring_o.start_left()
     sum_e.join()
+    links.drain(gathered)
     norm_mean, cross_row = norm_sums.finish()
     cross_mean = spread((cross_row - mean_row * norm_mean) * inv_row)
     norm_mean = spread(norm_mean)
@@ -719,6 +722,7 @@
             centred = value[:, cols] - row_avg[here, lanes] - normed * cross_avg[here, lanes]
             grad_input[rows, cols] = dg[y, rows, cols].astype(F32) + centred * inverse
     write(2, grad_input, grad_input_hbm)
+    links.drain()
     for head, group in enumerate((sum_0, sum_1)):
         low, high = group.finish()
         pieces[head * HEAD + QUERY] = low[:, 0:128]

time: 58.5 us -> 58.5 us (level)
  no operation moved by 1% of the time
where the time goes in v6:
time: 58.5 us; the launch traced here: 58.4 us
  Pallas kernels  57.7 us (99%)
  between operations  0.64 us (1%)
    pallas_call x1, Pallas kernels, shards(): pl.pallas_call(functools.partial(kernel, nz), out_shape=(jax.ShapeDtypeSt...  55.7 us
    pallas_call x1, Pallas kernels, shards(): pl.pallas_call(place_kernel, out_shape=[jax.ShapeDtypeStruct(r.shape, r.d...  2 us

profile of v6, /device:TPU:1, one launch (start us, length us, event | category | flops | bytes accessed | tf_op | source)
XLA Modules:
  0.0 58.4 jit_solution(14270724820385539713)
XLA Ops:
  0.6 55.7 %shard_map.84 = (bf16[512,256]{1,0:T(8,128)(2,1)}, f32[512,256]{1,0:T(8,128)}, f32[16,1024]{1,0:T(8,128)}, f32[16,256]{1,0:T(8,128)}) custom-call(bf16[512,256]{1,0:T(8,128)(2,1)} %history.1, bf16[512,256]{1,0:T(8,128)(2,1)} %out_grad.1, s32[1,8]{1,0:T(1,128)} %lengths_hbm.1, bf16[16,1024]{1,0:T(8,128)(2,1)} %w_in_hbm.1, bf16[16,256]{1,0:T(8,128)(2,1)} %bitcast.2), custom_call_target="tpu_custom_call" | custom-call | tf_op jit(solution)/shard_map/pallas_call | solution.py:769
  56.4 2.0 %shard_map.85 = (bf16[512,256]{1,0:T(8,128)(2,1)}, f32[512,256]{1,0:T(8,128)}, f32[16,1024]{1,0:T(8,128)}, f32[16,256]{1,0:T(8,128)}) custom-call(bf16[512,256]{1,0:T(8,128)(2,1)} %get-tuple-element.12.refs_0_, f32[512,256]{1,0:T(8,128)} %get-tuple-element.13.refs_1_, f32[16,1024]{1,0:T(8,128)} %get-tuple-element.14.refs_2_, f32[16,256]{1,0:T(8,128)} %get-tuple-element.15.refs_3_), custom_call_target="tpu_custom_call" | custom-call | tf_op jit(solution)/shard_map/pallas_call | solution.py:832
